TPU v7x, 32 devices: a whole 2x2x4 slice. The times are simulated.
32 devices in a mesh: sec: 4 (over z), row: 4 (over y, core), rad: 2 (over x).
Axes of the slice: x: 2, y: 2, z: 4, core: 2. Of those that a mesh axis runs over, the one named last changes fastest.
Arguments:
- state: float32 [5, 4, 16, 16, 512], P(None, 'sec', None, 'rad', 'row'), may hold values from -6 to 6
- volume: float32 [4, 16, 16, 512], P('sec', None, 'rad', 'row'), may hold values from 0.5 to 2
- face_axial: float32 [4, 16, 16, 512], P('sec', None, 'rad', 'row'), may hold values from 0.5 to 1.5
- face_radial: float32 [4, 16, 16, 512], P('sec', None, 'rad', 'row'), may hold values from 0.5 to 1.5
- face_circum: float32 [4, 16, 16, 512], P('sec', None, 'rad', 'row'), may hold values from 0.5 to 1.5
- viscosity: float32 [4, 16, 16, 512], P('sec', None, 'rad', 'row'), may hold values from 0.05 to 0.5
- flux_matrix: float32 [4, 3, 5, 5], P('sec'), may hold values from -2.5 to 2.5
- inflow_plane: float32 [5, 16, 512], P(None, 'rad', 'row'), may hold values from -6 to 6
- outflow_plane: float32 [5, 16, 512], P(None, 'rad', 'row'), may hold values from -6 to 6
- down_donors: int32 [4, 64], P('sec', ('row', 'rad')), may hold values from 0 to 63, each once within a row
- up_donors: int32 [4, 64], P('sec', ('row', 'rad')), may hold values from 0 to 63, each once within a row
- pressure_weight: float32 [5], replicated, may hold values from -3 to 3
- boundary_coupling: float32 [5], replicated, may hold values from -4 to 4
Outputs:
- advanced: float32 [5, 4, 16, 16, 512], P(None, 'sec', None, 'rad', 'row')
Inputs may be any that keep to these rules, and one draw needn't show every extreme that they name: `down_donors`: each row names each of the 64 tiles exactly once. `up_donors`: each row names each of the 64 tiles exactly once.
All inputs are finite; a program needn't handle non-finite values.
Results may differ from a plain program's by a relative error of at most 0.0001.
Values sent between devices are 32-bit elements; how exact they have to be, the bound alone decides.
A program may use at most 64 MiB of HBM per device.

v0:
```python
import jax
import jax.numpy as jnp
from jax import lax
from jax.sharding import PartitionSpec as P

STEPS = 4


time_step = 0.08


def padded_2(shard, sides, width):
    for axis, dim in sides:
        size, length = (lax.axis_size(axis), shard.shape[dim])
        up = [(i, (i + 1) % size) for i in range(size)]
        down = [(j, i) for i, j in up]
        last = lax.slice_in_dim(shard, length - width, length, axis=dim)
        first = lax.slice_in_dim(shard, 0, width, axis=dim)
        before = lax.ppermute(last, axis, up)
        after = lax.ppermute(first, axis, down)
        shard = jnp.concatenate([before, shard, after], axis=dim)
    return shard


def shifted(shard, axis, by):
    length = lax.axis_size(axis)
    pairs = [(i, i + by) for i in range(length) if 0 <= i + by < length]
    return lax.ppermute(shard, axis, pairs)


def to_tiles(plane):
    components, radial, beside_all = plane.shape
    shaped = plane.reshape(components, radial, beside_all // 128, 128)
    return shaped.transpose(1, 2, 0, 3).reshape(radial * (beside_all // 128), components, 128)


def from_tiles(tiles, radial, beside_all):
    components = tiles.shape[1]
    shaped = tiles.reshape(radial, beside_all // 128, components, 128)
    return shaped.transpose(2, 0, 1, 3).reshape(components, radial, beside_all)


def face_divergence(padded, face_area, viscous, matrix, direction):
    length = padded.shape[direction]
    lower_cells = lax.slice_in_dim(padded, 0, length - 1, axis=direction)
    upper_cells = lax.slice_in_dim(padded, 1, length, axis=direction)
    mixed = jnp.einsum(
        "uv,v...->u...", matrix, lower_cells + upper_cells, precision=lax.Precision.HIGHEST
    )
    fluxes = face_area * (0.5 * mixed - viscous * (upper_cells - lower_cells))
    return lax.slice_in_dim(fluxes, 1, length - 1, axis=direction) - lax.slice_in_dim(
        fluxes, 0, length - 2, axis=direction
    )


def select_tiles(piece, wanted):
    offsets = lax.broadcasted_iota(jnp.int32, (1, piece.shape[0]), 1)
    onehot = (wanted[:, None] == offsets).astype(jnp.float32)
    return jnp.einsum("tn,n...->t...", onehot, piece, precision=lax.Precision.HIGHEST)


def tile_pressure(weights, tiles):
    return jnp.einsum("v,tvc->tc", weights, tiles, precision=lax.Precision.HIGHEST)


def body(
    state,
    volume,
    face_axial,
    face_radial,
    face_circum,
    viscosity,
    flux_matrix,
    inflow_plane,
    outflow_plane,
    down_donors,
    up_donors,
    pressure_weight,
    boundary_coupling,
):
    section = lax.axis_index("sec")
    last_section = lax.axis_size("sec") - 1
    at_casing = lax.axis_index("rad") == lax.axis_size("rad") - 1
    field = state[:, 0]
    radial_cells = field.shape[2]
    around_cells = field.shape[3]
    cell_volume = volume[0]
    radial_face = face_radial[0]
    radial_rows = lax.broadcasted_iota(jnp.int32, radial_face.shape, 1)
    radial_face = jnp.where(
        jnp.logical_and(at_casing, radial_rows == radial_cells - 1), 0.0, radial_face
    )
    stacked = jnp.stack([radial_face, face_circum[0], viscosity[0]])
    rims = padded_2(stacked, (("row", 3), ("rad", 2)), 1)
    radial_area = rims[0, :, :-1, 1:-1]
    mu_radial = rims[2, :, :, 1:-1]
    nu_radial = 0.5 * (mu_radial[:, :-1] + mu_radial[:, 1:])
    circ_area = rims[1, :, 1:-1, :-1]
    mu_circ = rims[2, :, 1:-1, :]
    nu_circ = 0.5 * (mu_circ[:, :, :-1] + mu_circ[:, :, 1:])
    own_face = face_axial[0]
    axial_area = jnp.concatenate([own_face[:1], own_face], axis=0)
    own_mu = viscosity[0]
    mu_axial = jnp.concatenate([own_mu[:1], own_mu, own_mu[-1:]], axis=0)
    nu_axial = 0.5 * (mu_axial[:-1] + mu_axial[1:])
    down_local = down_donors[0]
    up_local = up_donors[0]
    inflow_tiles = to_tiles(inflow_plane)
    outflow_tiles = to_tiles(outflow_plane)
    matrices = flux_matrix[0]
    for step_index in range(STEPS):
        outlet_tiles = to_tiles(field[:, -1])
        inlet_tiles = to_tiles(field[:, 0])
        arrived = shifted(outlet_tiles, "sec", 1)
        donor_flow = jnp.where(section == 0, inflow_tiles, arrived)
        inlet_pressure = tile_pressure(pressure_weight, inlet_tiles)
        rising = shifted(inlet_pressure, "sec", -1)
        donor_beyond = jnp.where(
            section == last_section, tile_pressure(pressure_weight, outflow_tiles), rising
        )
        ghost_tiles = select_tiles(
            lax.all_gather(donor_flow, ("row", "rad"), axis=0, tiled=True), down_local
        )
        mapped_tiles = select_tiles(
            lax.all_gather(donor_beyond, ("row", "rad"), axis=0, tiled=True), up_local
        )
        inlet_ghost = from_tiles(ghost_tiles, radial_cells, around_cells)
        outlet = field[:, -1]
        own_pressure = jnp.einsum(
            "v,vjk->jk", pressure_weight, outlet, precision=lax.Precision.HIGHEST
        )
        outlet_ghost = (
            outlet + boundary_coupling[:, None, None] * (mapped_tiles - own_pressure)[None]
        )
        axial_padded = jnp.concatenate([inlet_ghost[:, None], field, outlet_ghost[:, None]], axis=1)
        halo_field = padded_2(field, (("row", 3), ("rad", 2)), 1)
        radial_padded = halo_field[:, :, :, 1:-1]
        circ_padded = halo_field[:, :, 1:-1, :]
        divergence = face_divergence(axial_padded, axial_area, nu_axial, matrices[0], 1)
        divergence = divergence + face_divergence(
            radial_padded, radial_area, nu_radial, matrices[1], 2
        )
        divergence = divergence + face_divergence(circ_padded, circ_area, nu_circ, matrices[2], 3)
        field = field - time_step / cell_volume * divergence
    return field[:, None]


def solution(mesh):
    in_specs = (
        P(None, "sec", None, "rad", "row"),
        P("sec", None, "rad", "row"),
        P("sec", None, "rad", "row"),
        P("sec", None, "rad", "row"),
        P("sec", None, "rad", "row"),
        P("sec", None, "rad", "row"),
        P("sec", None, None, None),
        P(None, "rad", "row"),
        P(None, "rad", "row"),
        P("sec", ("row", "rad")),
        P("sec", ("row", "rad")),
        P(),
        P(),
    )
    out_specs = P(None, "sec", None, "rad", "row")
    return jax.shard_map(body, mesh=mesh, in_specs=in_specs, out_specs=out_specs, check_vma=False)
```

profile of v0, /device:TPU:0, one launch (start us, length us, event | category | flops | bytes accessed | tf_op | source)
XLA Modules:
  0.0 192.4 jit_solution(16695189428555293026)
XLA Ops:
  0.0 1.0 copy.468
  1.2 2.5 %collective-permute-start.6 = (f32[5,16,8,1]{3,1,0,2:T(8,128)S(1)}, f32[5,16,8,1]{3,1,0,2:T(8,128)S(1)}, u32[]{:S(2)}, u32[]{:S(2)}) collective-permute-start(f32[5,16,8,1]{3,1,0,2:T(8,128)S(1)} %get-tuple-element.30), channel_id=1, source_target_pairs={{2,0},{4,2},{6,4},{0,6},{3,1},{5,3},{7,5},{1,7},{10,8},{12,10},{14... | collective-permute-start | bytes 7688 | tf_op jit(solution)/shard_map/ppermute | solution.py:20
  3.8 0.7 copy-done.1
  4.7 1.8 collective-permute-start.3
  7.4 1.4 collective-permute-start.1
  9.3 6.6 %collective-permute-done.3 = f32[3,16,8,1]{3,2,1,0:T(8,128)S(1)} collective-permute-done((f32[3,16,8,1]{3,2,1,0:T(8,128)S(1)}, f32[3,16,8,1]{3,2,1,0:T(8,128)S(1)}, u32[]{:S(2)}, u32[]{:S(2)}) %collective-permute-start.3) | collective-permute-done | bytes 1568 | tf_op jit(solution)/shard_map/ppermute | solution.py:20
  15.9 3.5 %collective-permute-start = (f32[8,5,128]{2,0,1:T(8,128)S(1)}, f32[8,5,128]{2,0,1:T(8,128)S(1)}, u32[]{:S(2)}, u32[]{:S(2)}) collective-permute-start(f32[8,5,128]{2,0,1:T(8,128)S(1)} %bitcast.291), channel_id=1, source_target_pairs={{0,8},{8,16},{16,24},{1,9},{9,17},{17,25},{2,10},{10,18},{18,26},{... | collective-permute-start | bytes 61448 | tf_op jit(solution)/shard_map/ppermute | solution.py:28
  20.2 1.6 collective-permute-start.9
  22.5 1.6 collective-permute-start.7
  24.3 1.4 fusion.6
  26.9 12.1 %all_gather.25 = f32[64,128]{1,0:T(8,128)S(1)} all-gather(f32[8,128]{1,0:T(8,128)S(1)} %broadcast_select_fusion.4), channel_id=1, replica_groups=mesh['sec'=4,'row'=4,'rad'=2] {'row','rad'}, dimensions={0}, use_global_device_ids=true | all-gather | bytes 36864 | tf_op jit(solution)/shard_map/all_gather | solution.py:125
  39.1 0.7 copy-done.12
  41.1 13.6 %all_gather.24 = f32[64,5,128]{2,0,1:T(8,128)S(1)} all-gather(f32[8,5,128]{2,0,1:T(8,128)S(1)} %bitcast_select_fusion.3), channel_id=1, replica_groups=mesh['sec'=4,'row'=4,'rad'=2] {'row','rad'}, dimensions={0}, use_global_device_ids=true | all-gather | bytes 184320 | tf_op jit(solution)/shard_map/all_gather | solution.py:122
  57.4 0.7 fusion.18
  58.4 0.7 copy-done.3
  59.5 0.9 collective-permute-start.13
  60.7 1.3 collective-permute-start.11
  62.0 4.5 %collective-permute-start.10 = (f32[8,5,128]{2,0,1:T(8,128)S(1)}, f32[8,5,128]{2,0,1:T(8,128)S(1)}, u32[]{:S(2)}, u32[]{:S(2)}) collective-permute-start(f32[8,5,128]{2,0,1:T(8,128)S(1)} %bitcast.293), channel_id=1, source_target_pairs={{0,8},{8,16},{16,24},{1,9},{9,17},{17,25},{2,10},{10,18},{18,26},{... | collective-permute-start | bytes 61448 | tf_op jit(solution)/shard_map/ppermute | solution.py:28
  66.6 1.1 collective-permute-done.13
  67.7 2.7 %collective-permute-done.12 = f32[5,16,8,1]{3,1,0,2:T(8,128)S(1)} collective-permute-done((f32[5,16,8,1]{3,1,0,2:T(8,128)S(1)}, f32[5,16,8,1]{3,1,0,2:T(8,128)S(1)}, u32[]{:S(2)}, u32[]{:S(2)}) %collective-permute-start.12) | collective-permute-done | bytes 2592 | tf_op jit(solution)/shard_map/ppermute | solution.py:19
  70.6 1.4 fusion.4
  72.6 1.8 collective-permute-start.15
  74.8 11.9 %all_gather.27 = f32[64,128]{1,0:T(8,128)S(1)} all-gather(f32[8,128]{1,0:T(8,128)S(1)} %broadcast_select_fusion.3), channel_id=1, replica_groups=mesh['sec'=4,'row'=4,'rad'=2] {'row','rad'}, dimensions={0}, use_global_device_ids=true | all-gather | bytes 36864 | tf_op jit(solution)/shard_map/all_gather | solution.py:125
  87.1 13.8 %all_gather.26 = f32[64,5,128]{2,0,1:T(8,128)S(1)} all-gather(f32[8,5,128]{2,0,1:T(8,128)S(1)} %bitcast_select_fusion.2), channel_id=1, replica_groups=mesh['sec'=4,'row'=4,'rad'=2] {'row','rad'}, dimensions={0}, use_global_device_ids=true | all-gather | bytes 184320 | tf_op jit(solution)/shard_map/all_gather | solution.py:122
  102.4 0.7 fusion.16
  103.8 0.8 collective-permute-start.19
  105.0 1.3 collective-permute-start.17
  106.3 4.5 %collective-permute-start.16 = (f32[8,5,128]{2,0,1:T(8,128)S(1)}, f32[8,5,128]{2,0,1:T(8,128)S(1)}, u32[]{:S(2)}, u32[]{:S(2)}) collective-permute-start(f32[8,5,128]{2,0,1:T(8,128)S(1)} %bitcast.294), channel_id=1, source_target_pairs={{0,8},{8,16},{16,24},{1,9},{9,17},{17,25},{2,10},{10,18},{18,26},{... | collective-permute-start | bytes 61448 | tf_op jit(solution)/shard_map/ppermute | solution.py:28
  110.8 0.9 collective-permute-done.19
  111.8 2.8 %collective-permute-done.18 = f32[5,16,8,1]{3,1,0,2:T(8,128)S(1)} collective-permute-done((f32[5,16,8,1]{3,1,0,2:T(8,128)S(1)}, f32[5,16,8,1]{3,1,0,2:T(8,128)S(1)}, u32[]{:S(2)}, u32[]{:S(2)}) %collective-permute-start.18) | collective-permute-done | bytes 2592 | tf_op jit(solution)/shard_map/ppermute | solution.py:19
  114.8 1.4 fusion.2
  116.4 0.8 collective-permute-start.20
  117.2 1.3 collective-permute-start.21
  119.0 11.7 %all_gather.29 = f32[64,128]{1,0:T(8,128)S(1)} all-gather(f32[8,128]{1,0:T(8,128)S(1)} %broadcast_select_fusion.2), channel_id=1, replica_groups=mesh['sec'=4,'row'=4,'rad'=2] {'row','rad'}, dimensions={0}, use_global_device_ids=true | all-gather | bytes 36864 | tf_op jit(solution)/shard_map/all_gather | solution.py:125
  131.0 13.7 %all_gather.28 = f32[64,5,128]{2,0,1:T(8,128)S(1)} all-gather(f32[8,5,128]{2,0,1:T(8,128)S(1)} %bitcast_select_fusion.1), channel_id=1, replica_groups=mesh['sec'=4,'row'=4,'rad'=2] {'row','rad'}, dimensions={0}, use_global_device_ids=true | all-gather | bytes 184320 | tf_op jit(solution)/shard_map/all_gather | solution.py:122
  146.3 0.7 fusion.14
  147.7 1.1 collective-permute-start.25
  149.1 1.3 collective-permute-start.23
  150.4 4.8 %collective-permute-start.22 = (f32[8,5,128]{2,0,1:T(8,128)S(1)}, f32[8,5,128]{2,0,1:T(8,128)S(1)}, u32[]{:S(2)}, u32[]{:S(2)}) collective-permute-start(f32[8,5,128]{2,0,1:T(8,128)S(1)} %bitcast.292), channel_id=1, source_target_pairs={{0,8},{8,16},{16,24},{1,9},{9,17},{17,25},{2,10},{10,18},{18,26},{... | collective-permute-start | bytes 61448 | tf_op jit(solution)/shard_map/ppermute | solution.py:28
  155.2 1.0 collective-permute-done.25
  156.1 2.5 %collective-permute-done.24 = f32[5,16,8,1]{3,1,0,2:T(8,128)S(1)} collective-permute-done((f32[5,16,8,1]{3,1,0,2:T(8,128)S(1)}, f32[5,16,8,1]{3,1,0,2:T(8,128)S(1)}, u32[]{:S(2)}, u32[]{:S(2)}) %collective-permute-start.24) | collective-permute-done | bytes 2592 | tf_op jit(solution)/shard_map/ppermute | solution.py:19
  158.8 1.4 fusion
  160.4 0.8 collective-permute-start.26
  161.2 1.3 collective-permute-start.27
  163.1 11.7 %all_gather.31 = f32[64,128]{1,0:T(8,128)S(1)} all-gather(f32[8,128]{1,0:T(8,128)S(1)} %broadcast_select_fusion.1), channel_id=1, replica_groups=mesh['sec'=4,'row'=4,'rad'=2] {'row','rad'}, dimensions={0}, use_global_device_ids=true | all-gather | bytes 36864 | tf_op jit(solution)/shard_map/all_gather | solution.py:125
  175.1 13.7 %all_gather.30 = f32[64,5,128]{2,0,1:T(8,128)S(1)} all-gather(f32[8,5,128]{2,0,1:T(8,128)S(1)} %bitcast_select_fusion), channel_id=1, replica_groups=mesh['sec'=4,'row'=4,'rad'=2] {'row','rad'}, dimensions={0}, use_global_device_ids=true | all-gather | bytes 184320 | tf_op jit(solution)/shard_map/all_gather | solution.py:122
  190.3 0.7 fusion.12
  191.5 0.8 copy.319
  (157 shorter events, 20.3 us)
Async XLA Ops:
  0.0 9.0 %copy-start = (f32[5,8,128]{2,1,0:T(8,128)S(1)}, f32[5,8,128]{2,1,0:T(8,128)}, u32[]{:S(2)}) copy-start(f32[5,8,128]{2,1,0:T(8,128)} %param.21) | copy-start | bytes 61444
  1.1 2.6 %copy-start.6 = (f32[1,16,8,128]{3,2,1,0:T(8,128)S(1)}, f32[1,16,8,128]{3,2,1,0:T(8,128)}, u32[]{:S(2)}) copy-start(f32[1,16,8,128]{3,2,1,0:T(8,128)} %param.16) | copy-start | bytes 196612
  1.2 20.6 %collective-permute-start.6 = (f32[5,16,8,1]{3,1,0,2:T(8,128)S(1)}, f32[5,16,8,1]{3,1,0,2:T(8,128)S(1)}, u32[]{:S(2)}, u32[]{:S(2)}) collective-permute-start(f32[5,16,8,1]{3,1,0,2:T(8,128)S(1)} %get-tuple-element.30), channel_id=1, source_target_pairs={{2,0},{4,2},{6,4},{0,6},{3,1},{5,3},{7,5},{1,7},{10,8},{12,10},{14... | collective-permute-start | bytes 7688 | tf_op jit(solution)/shard_map/ppermute | solution.py:20
  3.7 18.7 %collective-permute-start.5 = (f32[5,16,8,1]{3,1,0,2:T(8,128)S(1)}, f32[5,16,8,1]{3,1,0,2:T(8,128)S(1)}, u32[]{:S(2)}, u32[]{:S(2)}) collective-permute-start(f32[5,16,8,1]{3,1,0,2:T(8,128)S(1)} %get-tuple-element.29), channel_id=1, source_target_pairs={{0,2},{2,4},{4,6},{6,0},{1,3},{3,5},{5,7},{7,1},{8,10},{10,12},{12... | collective-permute-start | bytes 7688 | tf_op jit(solution)/shard_map/ppermute | solution.py:19
  3.7 0.8 copy-start.1
  3.7 0.9 copy-start.2
  4.7 11.2 %collective-permute-start.3 = (f32[3,16,8,1]{3,2,1,0:T(8,128)S(1)}, f32[3,16,8,1]{3,2,1,0:T(8,128)S(1)}, u32[]{:S(2)}, u32[]{:S(2)}) collective-permute-start(f32[3,16,8,1]{3,2,1,0:T(8,128)S(1)} %get-tuple-element.32), channel_id=1, source_target_pairs={{2,0},{4,2},{6,4},{0,6},{3,1},{5,3},{7,5},{1,7},{10,8},{12,10},{14... | collective-permute-start | bytes 4616 | tf_op jit(solution)/shard_map/ppermute | solution.py:20
  6.5 12.9 %collective-permute-start.2 = (f32[3,16,8,1]{3,2,1,0:T(8,128)S(1)}, f32[3,16,8,1]{3,2,1,0:T(8,128)S(1)}, u32[]{:S(2)}, u32[]{:S(2)}) collective-permute-start(f32[3,16,8,1]{3,2,1,0:T(8,128)S(1)} %get-tuple-element.31), channel_id=1, source_target_pairs={{0,2},{2,4},{4,6},{6,0},{1,3},{3,5},{5,7},{7,1},{8,10},{10,12},{12... | collective-permute-start | bytes 4616 | tf_op jit(solution)/shard_map/ppermute | solution.py:19
  6.5 2.3 %copy-start.11 = (f32[1,3,5,5]{3,0,2,1:T(1,128)S(1)}, f32[1,3,5,5]{3,0,2,1:T(1,128)}, u32[]{:S(2)}) copy-start(f32[1,3,5,5]{3,0,2,1:T(1,128)} %param.19) | copy-start | bytes 904
  6.5 0.7 copy-start.8
  7.2 2.0 %copy-start.5 = (f32[1,16,8,128]{3,2,1,0:T(8,128)S(1)}, f32[1,16,8,128]{3,2,1,0:T(8,128)}, u32[]{:S(2)}) copy-start(f32[1,16,8,128]{3,2,1,0:T(8,128)} %param.15) | copy-start | bytes 196612
  7.4 1.8 copy-start.7
  7.4 18.9 %collective-permute-start.1 = (f32[8,128]{1,0:T(8,128)S(1)}, f32[8,128]{1,0:T(8,128)S(1)}, u32[]{:S(2)}, u32[]{:S(2)}) collective-permute-start(f32[8,128]{1,0:T(8,128)S(1)} %bitcast.299), channel_id=1, source_target_pairs={{8,0},{16,8},{24,16},{9,1},{17,9},{25,17},{10,2},{18,10},{26,18},{... | collective-permute-start | bytes 12296 | tf_op jit(solution)/shard_map/ppermute | solution.py:28
  15.9 24.5 %collective-permute-start = (f32[8,5,128]{2,0,1:T(8,128)S(1)}, f32[8,5,128]{2,0,1:T(8,128)S(1)}, u32[]{:S(2)}, u32[]{:S(2)}) collective-permute-start(f32[8,5,128]{2,0,1:T(8,128)S(1)} %bitcast.291), channel_id=1, source_target_pairs={{0,8},{8,16},{16,24},{1,9},{9,17},{17,25},{2,10},{10,18},{18,26},{... | collective-permute-start | bytes 61448 | tf_op jit(solution)/shard_map/ppermute | solution.py:28
  20.2 36.4 %collective-permute-start.9 = (f32[3,16,1,130]{3,2,1,0:T(1,128)S(1)}, f32[3,16,1,130]{3,2,1,0:T(1,128)S(1)}, u32[]{:S(2)}, u32[]{:S(2)}) collective-permute-start(f32[3,16,1,130]{3,2,1,0:T(1,128)S(1)} %get-tuple-element.14), channel_id=1, source_target_pairs={{1,0},{0,1},{3,2},{2,3},{5,4},{4,5},{7,6},{6,7},{9,8},{8,9},{11,10... | collective-permute-start | bytes 74888 | tf_op jit(solution)/shard_map/ppermute | solution.py:20
  21.8 34.9 %collective-permute-start.4 = (f32[3,16,1,130]{3,2,1,0:T(1,128)S(1)}, f32[3,16,1,130]{3,2,1,0:T(1,128)S(1)}, u32[]{:S(2)}, u32[]{:S(2)}) collective-permute-start(f32[3,16,1,130]{3,2,1,0:T(1,128)S(1)} %get-tuple-element.13), channel_id=1, source_target_pairs={{0,1},{1,0},{2,3},{3,2},{4,5},{5,4},{6,7},{7,6},{8,9},{9,8},{10,11... | collective-permute-start | bytes 74888 | tf_op jit(solution)/shard_map/ppermute | solution.py:19
  22.5 34.6 %collective-permute-start.7 = (f32[5,16,1,130]{3,1,0,2:T(8,128)S(1)}, f32[5,16,1,130]{3,1,0,2:T(8,128)S(1)}, u32[]{:S(2)}, u32[]{:S(2)}) collective-permute-start(f32[5,16,1,130]{3,1,0,2:T(8,128)S(1)} %get-tuple-element.12), channel_id=1, source_target_pairs={{0,1},{1,0},{2,3},{3,2},{4,5},{5,4},{6,7},{7,6},{8,9},{9,8},{10,11... | collective-permute-start | bytes 124808 | tf_op jit(solution)/shard_map/ppermute | solution.py:19
  26.3 30.8 %collective-permute-start.8 = (f32[5,16,1,130]{3,1,0,2:T(8,128)S(1)}, f32[5,16,1,130]{3,1,0,2:T(8,128)S(1)}, u32[]{:S(2)}, u32[]{:S(2)}) collective-permute-start(f32[5,16,1,130]{3,1,0,2:T(8,128)S(1)} %get-tuple-element.11), channel_id=1, source_target_pairs={{1,0},{0,1},{3,2},{2,3},{5,4},{4,5},{7,6},{6,7},{9,8},{8,9},{11,10... | collective-permute-start | bytes 124808 | tf_op jit(solution)/shard_map/ppermute | solution.py:20
  39.1 0.7 copy-start.12
  39.7 0.7 copy-start.9
  40.4 0.7 copy-start.4
  54.7 0.7 copy-start.10
  58.1 1.0 copy-start.3
  59.5 8.1 %collective-permute-start.13 = (f32[5,16,8,1]{3,1,0,2:T(8,128)S(1)}, f32[5,16,8,1]{3,1,0,2:T(8,128)S(1)}, u32[]{:S(2)}, u32[]{:S(2)}) collective-permute-start(f32[5,16,8,1]{3,1,0,2:T(8,128)S(1)} %get-tuple-element.26), channel_id=1, source_target_pairs={{2,0},{4,2},{6,4},{0,6},{3,1},{5,3},{7,5},{1,7},{10,8},{12,10},{14... | collective-permute-start | bytes 7688 | tf_op jit(solution)/shard_map/ppermute | solution.py:20
  60.4 10.0 %collective-permute-start.12 = (f32[5,16,8,1]{3,1,0,2:T(8,128)S(1)}, f32[5,16,8,1]{3,1,0,2:T(8,128)S(1)}, u32[]{:S(2)}, u32[]{:S(2)}) collective-permute-start(f32[5,16,8,1]{3,1,0,2:T(8,128)S(1)} %get-tuple-element.25), channel_id=1, source_target_pairs={{0,2},{2,4},{4,6},{6,0},{1,3},{3,5},{5,7},{7,1},{8,10},{10,12},{12... | collective-permute-start | bytes 7688 | tf_op jit(solution)/shard_map/ppermute | solution.py:19
  60.7 14.1 %collective-permute-start.11 = (f32[8,128]{1,0:T(8,128)S(1)}, f32[8,128]{1,0:T(8,128)S(1)}, u32[]{:S(2)}, u32[]{:S(2)}) collective-permute-start(f32[8,128]{1,0:T(8,128)S(1)} %bitcast.305), channel_id=1, source_target_pairs={{8,0},{16,8},{24,16},{9,1},{17,9},{25,17},{10,2},{18,10},{26,18},{... | collective-permute-start | bytes 12296 | tf_op jit(solution)/shard_map/ppermute | solution.py:28
  62.0 25.0 %collective-permute-start.10 = (f32[8,5,128]{2,0,1:T(8,128)S(1)}, f32[8,5,128]{2,0,1:T(8,128)S(1)}, u32[]{:S(2)}, u32[]{:S(2)}) collective-permute-start(f32[8,5,128]{2,0,1:T(8,128)S(1)} %bitcast.293), channel_id=1, source_target_pairs={{0,8},{8,16},{16,24},{1,9},{9,17},{17,25},{2,10},{10,18},{18,26},{... | collective-permute-start | bytes 61448 | tf_op jit(solution)/shard_map/ppermute | solution.py:28
  72.2 29.9 %collective-permute-start.14 = (f32[5,16,1,130]{3,1,0,2:T(8,128)S(1)}, f32[5,16,1,130]{3,1,0,2:T(8,128)S(1)}, u32[]{:S(2)}, u32[]{:S(2)}) collective-permute-start(f32[5,16,1,130]{3,1,0,2:T(8,128)S(1)} %get-tuple-element.10), channel_id=1, source_target_pairs={{0,1},{1,0},{2,3},{3,2},{4,5},{5,4},{6,7},{7,6},{8,9},{9,8},{10,11... | collective-permute-start | bytes 124808 | tf_op jit(solution)/shard_map/ppermute | solution.py:19
  72.6 29.5 %collective-permute-start.15 = (f32[5,16,1,130]{3,1,0,2:T(8,128)S(1)}, f32[5,16,1,130]{3,1,0,2:T(8,128)S(1)}, u32[]{:S(2)}, u32[]{:S(2)}) collective-permute-start(f32[5,16,1,130]{3,1,0,2:T(8,128)S(1)} %get-tuple-element.9), channel_id=1, source_target_pairs={{1,0},{0,1},{3,2},{2,3},{5,4},{4,5},{7,6},{6,7},{9,8},{8,9},{11,10... | collective-permute-start | bytes 124808 | tf_op jit(solution)/shard_map/ppermute | solution.py:20
  103.8 8.0 %collective-permute-start.19 = (f32[5,16,8,1]{3,1,0,2:T(8,128)S(1)}, f32[5,16,8,1]{3,1,0,2:T(8,128)S(1)}, u32[]{:S(2)}, u32[]{:S(2)}) collective-permute-start(f32[5,16,8,1]{3,1,0,2:T(8,128)S(1)} %get-tuple-element.22), channel_id=1, source_target_pairs={{2,0},{4,2},{6,4},{0,6},{3,1},{5,3},{7,5},{1,7},{10,8},{12,10},{14... | collective-permute-start | bytes 7688 | tf_op jit(solution)/shard_map/ppermute | solution.py:20
  104.6 9.9 %collective-permute-start.18 = (f32[5,16,8,1]{3,1,0,2:T(8,128)S(1)}, f32[5,16,8,1]{3,1,0,2:T(8,128)S(1)}, u32[]{:S(2)}, u32[]{:S(2)}) collective-permute-start(f32[5,16,8,1]{3,1,0,2:T(8,128)S(1)} %get-tuple-element.21), channel_id=1, source_target_pairs={{0,2},{2,4},{4,6},{6,0},{1,3},{3,5},{5,7},{7,1},{8,10},{10,12},{12... | collective-permute-start | bytes 7688 | tf_op jit(solution)/shard_map/ppermute | solution.py:19
  105.0 14.0 %collective-permute-start.17 = (f32[8,128]{1,0:T(8,128)S(1)}, f32[8,128]{1,0:T(8,128)S(1)}, u32[]{:S(2)}, u32[]{:S(2)}) collective-permute-start(f32[8,128]{1,0:T(8,128)S(1)} %bitcast.306), channel_id=1, source_target_pairs={{8,0},{16,8},{24,16},{9,1},{17,9},{25,17},{10,2},{18,10},{26,18},{... | collective-permute-start | bytes 12296 | tf_op jit(solution)/shard_map/ppermute | solution.py:28
  106.3 24.7 %collective-permute-start.16 = (f32[8,5,128]{2,0,1:T(8,128)S(1)}, f32[8,5,128]{2,0,1:T(8,128)S(1)}, u32[]{:S(2)}, u32[]{:S(2)}) collective-permute-start(f32[8,5,128]{2,0,1:T(8,128)S(1)} %bitcast.294), channel_id=1, source_target_pairs={{0,8},{8,16},{16,24},{1,9},{9,17},{17,25},{2,10},{10,18},{18,26},{... | collective-permute-start | bytes 61448 | tf_op jit(solution)/shard_map/ppermute | solution.py:28
  116.4 29.6 %collective-permute-start.20 = (f32[5,16,1,130]{3,1,0,2:T(8,128)S(1)}, f32[5,16,1,130]{3,1,0,2:T(8,128)S(1)}, u32[]{:S(2)}, u32[]{:S(2)}) collective-permute-start(f32[5,16,1,130]{3,1,0,2:T(8,128)S(1)} %get-tuple-element.8), channel_id=1, source_target_pairs={{0,1},{1,0},{2,3},{3,2},{4,5},{5,4},{6,7},{7,6},{8,9},{9,8},{10,11... | collective-permute-start | bytes 124808 | tf_op jit(solution)/shard_map/ppermute | solution.py:19
  117.2 28.8 %collective-permute-start.21 = (f32[5,16,1,130]{3,1,0,2:T(8,128)S(1)}, f32[5,16,1,130]{3,1,0,2:T(8,128)S(1)}, u32[]{:S(2)}, u32[]{:S(2)}) collective-permute-start(f32[5,16,1,130]{3,1,0,2:T(8,128)S(1)} %get-tuple-element.7), channel_id=1, source_target_pairs={{1,0},{0,1},{3,2},{2,3},{5,4},{4,5},{7,6},{6,7},{9,8},{8,9},{11,10... | collective-permute-start | bytes 124808 | tf_op jit(solution)/shard_map/ppermute | solution.py:20
  147.7 8.5 %collective-permute-start.25 = (f32[5,16,8,1]{3,1,0,2:T(8,128)S(1)}, f32[5,16,8,1]{3,1,0,2:T(8,128)S(1)}, u32[]{:S(2)}, u32[]{:S(2)}) collective-permute-start(f32[5,16,8,1]{3,1,0,2:T(8,128)S(1)} %get-tuple-element.18), channel_id=1, source_target_pairs={{2,0},{4,2},{6,4},{0,6},{3,1},{5,3},{7,5},{1,7},{10,8},{12,10},{14... | collective-permute-start | bytes 7688 | tf_op jit(solution)/shard_map/ppermute | solution.py:20
  148.7 9.9 %collective-permute-start.24 = (f32[5,16,8,1]{3,1,0,2:T(8,128)S(1)}, f32[5,16,8,1]{3,1,0,2:T(8,128)S(1)}, u32[]{:S(2)}, u32[]{:S(2)}) collective-permute-start(f32[5,16,8,1]{3,1,0,2:T(8,128)S(1)} %get-tuple-element.17), channel_id=1, source_target_pairs={{0,2},{2,4},{4,6},{6,0},{1,3},{3,5},{5,7},{7,1},{8,10},{10,12},{12... | collective-permute-start | bytes 7688 | tf_op jit(solution)/shard_map/ppermute | solution.py:19
  149.1 14.0 %collective-permute-start.23 = (f32[8,128]{1,0:T(8,128)S(1)}, f32[8,128]{1,0:T(8,128)S(1)}, u32[]{:S(2)}, u32[]{:S(2)}) collective-permute-start(f32[8,128]{1,0:T(8,128)S(1)} %bitcast.304), channel_id=1, source_target_pairs={{8,0},{16,8},{24,16},{9,1},{17,9},{25,17},{10,2},{18,10},{26,18},{... | collective-permute-start | bytes 12296 | tf_op jit(solution)/shard_map/ppermute | solution.py:28
  150.4 24.7 %collective-permute-start.22 = (f32[8,5,128]{2,0,1:T(8,128)S(1)}, f32[8,5,128]{2,0,1:T(8,128)S(1)}, u32[]{:S(2)}, u32[]{:S(2)}) collective-permute-start(f32[8,5,128]{2,0,1:T(8,128)S(1)} %bitcast.292), channel_id=1, source_target_pairs={{0,8},{8,16},{16,24},{1,9},{9,17},{17,25},{2,10},{10,18},{18,26},{... | collective-permute-start | bytes 61448 | tf_op jit(solution)/shard_map/ppermute | solution.py:28
  160.4 29.6 %collective-permute-start.26 = (f32[5,16,1,130]{3,1,0,2:T(8,128)S(1)}, f32[5,16,1,130]{3,1,0,2:T(8,128)S(1)}, u32[]{:S(2)}, u32[]{:S(2)}) collective-permute-start(f32[5,16,1,130]{3,1,0,2:T(8,128)S(1)} %get-tuple-element.6), channel_id=1, source_target_pairs={{0,1},{1,0},{2,3},{3,2},{4,5},{5,4},{6,7},{7,6},{8,9},{9,8},{10,11... | collective-permute-start | bytes 124808 | tf_op jit(solution)/shard_map/ppermute | solution.py:19
  161.2 28.8 %collective-permute-start.27 = (f32[5,16,1,130]{3,1,0,2:T(8,128)S(1)}, f32[5,16,1,130]{3,1,0,2:T(8,128)S(1)}, u32[]{:S(2)}, u32[]{:S(2)}) collective-permute-start(f32[5,16,1,130]{3,1,0,2:T(8,128)S(1)} %get-tuple-element.5), channel_id=1, source_target_pairs={{1,0},{0,1},{3,2},{2,3},{5,4},{4,5},{7,6},{6,7},{9,8},{8,9},{11,10... | collective-permute-start | bytes 124808 | tf_op jit(solution)/shard_map/ppermute | solution.py:20
where the time goes:
time: 193 us; the launch traced here: 192 us
  blocking collectives  102 us (53%)
  starting transfers between devices  40.2 us (21%)
  waiting for transfers between devices  17.6 us (9%)
  matrix products  14.2 us (7%)
  other arithmetic  9.54 us (5%)
  local copies, waits for them, and re-layouts  7.64 us (4%)
    all_gather x4, blocking collectives, body(): lax.all_gather(donor_flow, ('row', 'rad'), axis=0, tiled=True)  54.8 us
    all_gather x4, blocking collectives, body(): lax.all_gather(donor_beyond, ('row', 'rad'), axis=0, tiled=True)  47.4 us
    ppermute x8, starting transfers between devices, shifted(): return lax.ppermute(shard, axis, pairs)  22.6 us
    ppermute x10, starting transfers between devices, padded_2(): after = lax.ppermute(first, axis, down)  13.5 us
    dot_general x12, matrix products, face_divergence(): jnp.einsum('uv,v...->u...', matrix, lower_cells + upper_cells, precision=...  11.3 us
    ppermute x10, waiting for transfers between devices, padded_2(): after = lax.ppermute(first, axis, down)  9.59 us
    ppermute x10, waiting for transfers between devices, padded_2(): before = lax.ppermute(last, axis, up)  8.01 us
    unnamed x27, local copies, waits for them, and re-layouts  5.61 us
  transfers between devices with their start and end apart: 28, of which 7 were waited for; matrix products, arithmetic and copies ran while one was open for 10% of the time, Pallas kernels for 0%

commit v1 on v0

v1 whole, which is shorter than its diff:
```python
import functools

import jax
import jax.numpy as jnp
from jax import lax
from jax.experimental import pallas as pl
from jax.experimental.pallas import tpu as pltpu
from jax.sharding import PartitionSpec as P

STEPS = 4


time_step = 0.08

MESH = pl.DeviceIdType.MESH
N_COEF = 16


def kernel(
    sizes,
    state,
    volume,
    face_axial,
    face_radial,
    face_circum,
    viscosity,
    matrix,
    inflow,
    outflow,
    down,
    up,
    weight,
    coupling,
    out,
    field,
    coef,
    flow,
    flow_send,
    press,
    press_send,
    ghost,
    mapped,
    row_in,
    row_out,
    rad_in,
    rad_out,
    rad_in0,
    rad_out0,
    flow_ss,
    flow_rs,
    press_ss,
    press_rs,
    edge_ss,
    row_ss,
    row_rs,
    rad_ss,
    rad_rs,
):
    n_sec, n_row, n_rad, nv, nx, nr, lanes = sizes
    group = n_row * n_rad
    planes = nv * nx
    block = nv * nr
    sec, row, rad = lax.axis_index("sec"), lax.axis_index("row"), lax.axis_index("rad")
    mine = row * n_rad + rad
    first, last = sec == 0, sec == n_sec - 1
    floor, casing = rad == 0, rad == n_rad - 1
    right, left = lax.rem(row + 1, n_row), lax.rem(row + n_row - 1, n_row)
    lane = lax.broadcasted_iota(jnp.int32, (nr, lanes), 1)
    sub = lax.broadcasted_iota(jnp.int32, (nr, lanes), 0)

    def device(section, index):
        return {"sec": section, "row": lax.div(index, n_rad), "rad": lax.rem(index, n_rad)}

    def each(action, skip_self=False):
        def one(i):
            index = lax.rem(mine + i, group)
            action(index)

        start = 1 if skip_self else 0
        if group <= 16:
            for i in range(start, group):
                one(i)
        else:
            pl.loop(start, group)(one)

    def send(src, dst, send_sem, recv_sem, to):
        pltpu.make_async_remote_copy(
            src_ref=src,
            dst_ref=dst,
            send_sem=send_sem,
            recv_sem=recv_sem,
            device_id=to,
            device_id_type=MESH,
        ).start()

    def wait(ref, sem):
        pltpu.make_async_copy(ref, ref, sem).wait()

    def rows(index):
        if isinstance(index, int):
            return pl.ds(index * nr, nr)
        return pl.ds(pl.multiple_of(index * nr, nr), nr)

    barrier = pltpu.get_barrier_semaphore()

    def greet(to):
        pl.semaphore_signal(barrier, inc=1, device_id=to, device_id_type=MESH)

    greet({"row": left})
    greet({"row": right})

    @pl.when(jnp.logical_not(floor))
    def _():
        greet({"rad": rad - 1})

    @pl.when(jnp.logical_not(casing))
    def _():
        greet({"rad": rad + 1})

    @pl.when(jnp.logical_not(first))
    def _():
        each(lambda index: greet(device(sec - 1, index)))

    @pl.when(jnp.logical_not(last))
    def _():
        each(lambda index: greet(device(sec + 1, index)))

    @pl.when(first)
    def _():
        each(lambda index: greet(device(sec, index)), True)

    @pl.when(last)
    def _():
        each(lambda index: greet(device(sec, index)), True)

    def pressure_of(values):
        total = weight[0] * values[0]
        for v in range(1, nv):
            total = total + weight[v] * values[v]
        return total

    press_send[0] = pressure_of([state[rows(v * nx)] for v in range(nv)])
    press_send[STEPS] = pressure_of([outflow[rows(v)] for v in range(nv)])
    for v in range(nv):
        flow_send[0, rows(v)] = state[rows(v * nx + nx - 1)]

    def pack_one(packs, value, index):
        to_left, to_right = packs
        to_left = jnp.where(lane == index, pltpu.roll(value, index, 1), to_left)
        to_right = jnp.where(lane == index, pltpu.roll(value, index + 1, 1), to_right)
        return to_left, to_right

    blank = jnp.zeros((nr, lanes), jnp.float32)

    def pack_start(x, packs):
        for v in range(nv):
            packs = pack_one(packs, state[rows(v * nx + x)], v * nx + x)
        packs = pack_one(packs, viscosity[rows(x)], planes + x)
        return pack_one(packs, face_circum[rows(x)], planes + nx + x)

    packs = lax.fori_loop(0, nx, pack_start, (blank, blank))
    row_out[0, 0, 0] = packs[0]
    row_out[0, 0, 1] = packs[1]
    for side, edge in ((0, 0), (1, nr - 1)):
        rad_out[0, side, pl.ds(0, planes)] = state[pl.ds(edge, planes, stride=nr)]
        rad_out[0, side, pl.ds(planes, nx)] = viscosity[pl.ds(edge, nx, stride=nr)]
        rad_out[0, side, pl.ds(planes + nx, nx)] = face_radial[pl.ds(edge, nx, stride=nr)]
    for v in range(nv):
        for slot in range(2):
            field[slot, rows(v * nx)] = blank
    for step in range(STEPS):
        for side in range(2):
            rad_out0[step, side] = blank

    @pl.when(floor)
    def _():
        for step in range(STEPS):
            rad_in[step, 0] = jnp.zeros(rad_in.shape[2:], jnp.float32)
            rad_in0[step, 0] = blank

    @pl.when(casing)
    def _():
        for step in range(STEPS):
            rad_in[step, 1] = jnp.zeros(rad_in.shape[2:], jnp.float32)
            rad_in0[step, 1] = blank

    one = jnp.int32(1)
    zero = jnp.int32(0)
    inner = group + group - jnp.where(jnp.logical_or(first, last), one, zero)
    inner = inner - (1 if n_sec == 1 else 0)
    beside = jnp.where(floor, zero, one) + jnp.where(casing, zero, one)
    pl.semaphore_wait(barrier, 2 + inner + beside)

    def send_flow(step):
        @pl.when(jnp.logical_not(last))
        def _():
            each(
                lambda index: send(
                    flow_send.at[step],
                    flow[step].at[mine],
                    flow_ss.at[step],
                    flow_rs.at[step],
                    device(sec + 1, index),
                )
            )

    def send_press(step):
        @pl.when(jnp.logical_not(first))
        def _():
            each(
                lambda index: send(
                    press_send.at[step],
                    press[step].at[mine],
                    press_ss.at[step],
                    press_rs.at[step],
                    device(sec - 1, index),
                )
            )

    def send_rows(step, part):
        for side, to in ((0, left), (1, right)):
            send(
                row_out.at[step, part, side],
                row_in.at[step, part, 1 - side],
                row_ss.at[step, part, side],
                row_rs.at[step, part, 1 - side],
                {"row": to},
            )

    def rad_refs(step, part, side):
        if part:
            return rad_out0.at[step, side], rad_in0.at[step, 1 - side]
        count = planes if step else planes + 2 * nx
        return (
            rad_out.at[step, side, pl.ds(0, count)],
            rad_in.at[step, 1 - side, pl.ds(0, count)],
        )

    def send_rads(step, part):
        for side, edge, to in ((0, floor, rad - 1), (1, casing, rad + 1)):

            @pl.when(jnp.logical_not(edge))
            def _(side=side, to=to):
                src, dst = rad_refs(step, part, side)
                send(
                    src,
                    dst,
                    rad_ss.at[step, part, side],
                    rad_rs.at[step, part, 1 - side],
                    {"rad": to},
                )

    def wait_beside(step, part):
        for side, edge in ((0, floor), (1, casing)):
            wait(row_in.at[step, part, side], row_rs.at[step, part, side])

            @pl.when(jnp.logical_not(edge))
            def _(side=side):
                wait(rad_refs(step, part, 1 - side)[1], rad_rs.at[step, part, side])

    send_rows(0, 0)
    send_rads(0, 0)
    send_press(0)

    @pl.when(last)
    def _():
        each(
            lambda index: send(
                press_send.at[STEPS],
                press[0].at[mine],
                edge_ss.at[1],
                press_rs.at[0],
                device(sec, index),
            ),
            True,
        )
        pltpu.make_async_copy(press_send.at[STEPS], press[0].at[mine], press_rs.at[0]).start()

    @pl.when(first)
    def _():
        each(
            lambda index: send(
                inflow, flow[0].at[mine], edge_ss.at[0], flow_rs.at[0], device(sec, index)
            ),
            True,
        )
        pltpu.make_async_copy(inflow, flow[0].at[mine], flow_rs.at[0]).start()

    send_flow(0)

    wait_beside(0, 0)

    def lower_lane(value, packed, index):
        return jnp.where(
            lane == 0, pltpu.roll(packed, lax.rem(lanes - index, lanes), 1), pltpu.roll(value, 1, 1)
        )

    def upper_lane(value, packed, index):
        return jnp.where(
            lane == lanes - 1,
            pltpu.roll(packed, lanes - 1 - index, 1),
            pltpu.roll(value, lanes - 1, 1),
        )

    def lower_sub(value, edge_row):
        return jnp.where(sub == 0, edge_row, pltpu.roll(value, 1, 0))

    def upper_sub(value, edge_row):
        return jnp.where(sub == nr - 1, edge_row, pltpu.roll(value, nr - 1, 0))

    wall = jnp.logical_and(casing, sub == nr - 1)

    def prepare(x, carry):
        below, above = jnp.maximum(x - 1, 0), jnp.minimum(x + 1, nx - 1)
        scale = time_step / volume[rows(x)]
        half = 0.5 * scale
        mu = viscosity[rows(x)]
        area = face_radial[rows(x)]
        area = jnp.where(wall, 0.0, area)
        around = face_circum[rows(x)]
        from_left, from_right = row_in[0, 0, 0], row_in[0, 0, 1]
        lower = (
            (face_axial[rows(below)], viscosity[rows(below)]),
            (
                lower_sub(area, rad_in[0, 0, pl.ds(planes + nx + x, 1)]),
                lower_sub(mu, rad_in[0, 0, pl.ds(planes + x, 1)]),
            ),
            (
                lower_lane(around, from_left, planes + nx + x),
                lower_lane(mu, from_left, planes + x),
            ),
        )
        upper = (
            (face_axial[rows(x)], viscosity[rows(above)]),
            (area, upper_sub(mu, rad_in[0, 1, pl.ds(planes + x, 1)])),
            (around, upper_lane(mu, from_right, planes + x)),
        )
        keep = jnp.ones_like(mu)
        for d in range(3):
            area_l, mu_l = lower[d]
            area_u, mu_u = upper[d]
            mix_l, mix_u = half * area_l, half * area_u
            spread_l, spread_u = mix_l * (mu_l + mu), mix_u * (mu_u + mu)
            keep = keep - (spread_l + spread_u)
            coef[5 * d, rows(x)] = mix_u
            coef[5 * d + 1, rows(x)] = mix_u - mix_l
            coef[5 * d + 2, rows(x)] = mix_l
            coef[5 * d + 3, rows(x)] = spread_u
            coef[5 * d + 4, rows(x)] = spread_l
        coef[N_COEF - 1, rows(x)] = keep
        return carry

    lax.fori_loop(0, nx, prepare, 0)

    def advance(x, centre, before, after, packed, edge_rows):
        from_left, from_right = packed
        c = [coef[k, rows(x)] for k in range(N_COEF)]
        mixed, fresh = [], []
        for v in range(nv):
            index = v * nx + x
            mid = centre[v]
            below, above = edge_rows(v)
            pairs = (
                (before[v], after[v]),
                (lower_sub(mid, below), upper_sub(mid, above)),
                (lower_lane(mid, from_left, index), upper_lane(mid, from_right, index)),
            )
            kept = c[N_COEF - 1] * mid
            for d, (lo, hi) in enumerate(pairs):
                mixed.append(c[5 * d] * hi + c[5 * d + 1] * mid - c[5 * d + 2] * lo)
                kept = kept + (c[5 * d + 3] * hi + c[5 * d + 4] * lo)
            fresh.append(kept)
        result = []
        for u in range(nv):
            total = None
            for d in range(3):
                for v in range(nv):
                    term = matrix[0, d, u, v] * mixed[3 * v + d]
                    total = term if total is None else total + term
            result.append(fresh[u] - total)
        return result

    for step in range(STEPS):
        final = step == STEPS - 1
        src = state if step == 0 else field.at[(step - 1) % 2]
        dst = out if final else field.at[step % 2]
        if step:
            wait_beside(step, 0)

        def plane(x):
            return [src[rows(v * nx + x)] for v in range(nv)]

        def keep_plane(x, values):
            for v in range(nv):
                dst[rows(v * nx + x)] = values[v]

        def pack_plane(x, values, packs):
            if final:
                return packs
            for v in range(nv):
                packs = pack_one(packs, values[v], v * nx + x)
            return packs

        def edge_rows_at(x, step=step):
            def edge_rows(v):
                at = pl.ds(v * nx + x, 1)
                return rad_in[step, 0, at], rad_in[step, 1, at]

            return edge_rows

        def inside(x, packs):
            packed = row_in[step, 0, 0], row_in[step, 0, 1]
            values = advance(
                x, plane(x), plane(x - 1), plane(x + 1), packed, edge_rows_at(x)
            )
            keep_plane(x, values)
            return pack_plane(x, values, packs)

        def inside_two(i, packs):
            x = 1 + 2 * i
            return inside(x + 1, inside(x, packs))

        pairs = (nx - 2) // 2
        packs = lax.fori_loop(0, pairs, inside_two, (blank, blank))
        for x in range(1 + 2 * pairs, nx - 1):
            packs = inside(x, packs)

        def take_press(step=step):
            wait(press[step], press_rs.at[step])
            for a in range(nr):
                donor = up[0, a]
                at = pl.ds(lax.rem(donor, nr), 1)
                mapped[pl.ds(a, 1)] = press[step][lax.div(donor, nr), at]

        if step:
            pl.when(jnp.logical_not(last))(take_press)
        else:
            take_press()
        centre = plane(nx - 1)
        gap = mapped[...] - pressure_of(centre)
        after = [centre[v] + coupling[v] * gap for v in range(nv)]
        packed = row_in[step, 0, 0], row_in[step, 0, 1]
        values = advance(
            nx - 1, centre, plane(nx - 2), after, packed, edge_rows_at(nx - 1)
        )
        keep_plane(nx - 1, values)
        if not final:
            for v in range(nv):
                flow_send[step + 1, rows(v)] = values[v]
            send_flow(step + 1)
            packs = pack_plane(nx - 1, values, packs)
            row_out[step + 1, 0, 0] = packs[0]
            row_out[step + 1, 0, 1] = packs[1]
            send_rows(step + 1, 0)
            for side, edge in ((0, 0), (1, nr - 1)):
                rad_out[step + 1, side, pl.ds(0, planes)] = dst[pl.ds(edge, planes, stride=nr)]
            send_rads(step + 1, 0)

        def take_flow(step=step):
            wait(flow[step], flow_rs.at[step])
            for a in range(nr):
                donor = down[0, a]
                owner, base = lax.div(donor, nr), lax.rem(donor, nr)
                for v in range(nv):
                    ghost[pl.ds(v * nr + a, 1)] = flow[step][owner, pl.ds(v * nr + base, 1)]

        if step:
            wait_beside(step, 1)
            pl.when(jnp.logical_not(first))(take_flow)

            def edge_rows(v, step=step):
                at = pl.ds(v, 1)
                return rad_in0[step, 0, at], rad_in0[step, 1, at]

            packed = row_in[step, 1, 0], row_in[step, 1, 1]
        else:
            take_flow()
            edge_rows = edge_rows_at(0)
        before = [ghost[rows(v)] for v in range(nv)]
        values = advance(0, plane(0), before, plane(1), packed, edge_rows)
        keep_plane(0, values)
        if not final:
            press_send[step + 1] = pressure_of(values)
            send_press(step + 1)
            packs = pack_plane(0, values, (blank, blank))
            row_out[step + 1, 1, 0] = packs[0]
            row_out[step + 1, 1, 1] = packs[1]
            send_rows(step + 1, 1)
            for v in range(nv):
                rad_out0[step + 1, 0, pl.ds(v, 1)] = values[v][:1]
                rad_out0[step + 1, 1, pl.ds(v, 1)] = values[v][nr - 1 :]
            send_rads(step + 1, 1)

    for step in range(STEPS):
        for part in range(2 if step else 1):
            for side, edge in ((0, floor), (1, casing)):
                wait(row_out.at[step, part, side], row_ss.at[step, part, side])

                @pl.when(jnp.logical_not(edge))
                def _(step=step, part=part, side=side):
                    wait(rad_refs(step, part, side)[0], rad_ss.at[step, part, side])

    @pl.when(jnp.logical_not(last))
    def _():
        for step in range(STEPS):
            wait(flow[step], flow_ss.at[step])

    @pl.when(jnp.logical_not(first))
    def _():
        for step in range(STEPS):
            wait(press[step], press_ss.at[step])

    @pl.when(first)
    def _():
        wait(flow[0].at[pl.ds(0, group - 1)], edge_ss.at[0])

    @pl.when(last)
    def _():
        wait(press[0].at[pl.ds(0, group - 1)], edge_ss.at[1])


def body(
    n_sec,
    n_row,
    n_rad,
    state,
    volume,
    face_axial,
    face_radial,
    face_circum,
    viscosity,
    flux_matrix,
    inflow_plane,
    outflow_plane,
    down_donors,
    up_donors,
    pressure_weight,
    boundary_coupling,
):
    nv, _, nx, nr, lanes = state.shape
    group = n_row * n_rad
    planes, block = nv * nx, nv * nr
    held = planes + 2 * nx

    def flat(array):
        return array.reshape(-1, lanes)

    def vmem(*shape):
        return pltpu.VMEM(shape, jnp.float32)

    dma = pltpu.SemaphoreType.DMA
    in_vmem = pl.BlockSpec(memory_space=pltpu.VMEM)
    in_smem = pl.BlockSpec(memory_space=pltpu.SMEM)
    result = pl.pallas_call(
        functools.partial(kernel, (n_sec, n_row, n_rad, nv, nx, nr, lanes)),
        out_shape=jax.ShapeDtypeStruct((planes * nr, lanes), jnp.float32),
        in_specs=[in_vmem] * 6 + [in_smem] + [in_vmem] * 2 + [in_smem] * 4,
        out_specs=in_vmem,
        scratch_shapes=[
            vmem(2, planes * nr, lanes),
            vmem(N_COEF, nx * nr, lanes),
            [vmem(group, block, lanes)] * STEPS,
            vmem(STEPS, block, lanes),
            [vmem(group, nr, lanes)] * STEPS,
            vmem(STEPS + 1, nr, lanes),
            vmem(block, lanes),
            vmem(nr, lanes),
            vmem(STEPS, 2, 2, nr, lanes),
            vmem(STEPS, 2, 2, nr, lanes),
            vmem(STEPS, 2, held, lanes),
            vmem(STEPS, 2, held, lanes),
            vmem(STEPS, 2, nr, lanes),
            vmem(STEPS, 2, nr, lanes),
            dma((STEPS,)),
            dma((STEPS,)),
            dma((STEPS,)),
            dma((STEPS,)),
            dma((2,)),
            dma((STEPS, 2, 2)),
            dma((STEPS, 2, 2)),
            dma((STEPS, 2, 2)),
            dma((STEPS, 2, 2)),
        ],
        compiler_params=pltpu.CompilerParams(
            collective_id=0, has_side_effects=True, vmem_limit_bytes=32 * 1024 * 1024
        ),
        name="coupled_steps",
    )(
        flat(state),
        flat(volume),
        flat(face_axial),
        flat(face_radial),
        flat(face_circum),
        flat(viscosity),
        flux_matrix,
        flat(inflow_plane),
        flat(outflow_plane),
        down_donors,
        up_donors,
        pressure_weight,
        boundary_coupling,
    )
    return result.reshape(state.shape)


def solution(mesh):
    in_specs = (
        P(None, "sec", None, "rad", "row"),
        P("sec", None, "rad", "row"),
        P("sec", None, "rad", "row"),
        P("sec", None, "rad", "row"),
        P("sec", None, "rad", "row"),
        P("sec", None, "rad", "row"),
        P("sec", None, None, None),
        P(None, "rad", "row"),
        P(None, "rad", "row"),
        P("sec", ("row", "rad")),
        P("sec", ("row", "rad")),
        P(),
        P(),
    )
    out_specs = P(None, "sec", None, "rad", "row")
    sizes = tuple(mesh.shape[name] for name in ("sec", "row", "rad"))
    return jax.shard_map(
        functools.partial(body, *sizes),
        mesh=mesh,
        in_specs=in_specs,
        out_specs=out_specs,
        check_vma=False,
    )
```

time: 193 us -> 37.5 us (0.19)
  blocking collectives: 102 us -> 0 us
  starting transfers between devices: 40.2 us -> 0 us
  Pallas kernels: 0 us -> 29.6 us
  waiting for transfers between devices: 17.6 us -> 0 us
  matrix products: 14.2 us -> 0 us
  other arithmetic: 9.54 us -> 0 us
    all_gather x8 -> x0, blocking collectives: 102 us -> none  [the longest x4 54.8 us: body(): lax.all_gather(donor_flow, ('row', 'rad'), axis=0, tiled=True)]
    ppermute x28 -> x0, starting transfers between devices: 40.2 us -> none  [the longest x8 22.6 us: shifted(): return lax.ppermute(shard, axis, pairs)]
    pallas_call x0 -> x1, Pallas kernels: none -> 29.6 us  [body(): pl.pallas_call(functools.partial(kernel, (n_sec, n_row, n_rad, nv, nx, nr...]
    ppermute x28 -> x0, waiting for transfers between devices: 17.6 us -> none  [the longest x10 9.59 us: padded_2(): after = lax.ppermute(first, axis, down)]
    dot_general x29 -> x0, matrix products: 14.2 us -> none  [the longest x12 11.3 us: face_divergence(): jnp.einsum('uv,v...->u...', matrix, lower_cells + upper_cells, precision=...]
    mul x18 -> x0, other arithmetic: 4.76 us -> none  [the longest x14 4.61 us: face_divergence(): fluxes = face_area * (0.5 * mixed - viscous * (upper_cells - lower_cells))]
    add x16 -> x0, other arithmetic: 2.64 us -> none  [the longest x12 2.26 us: face_divergence(): lower_cells + upper_cells]
    unnamed x27 -> x26, local copies, waits for them, and re-layouts: 5.61 us -> 7.4 us
  transfers between devices with their start and end apart: 28 -> 0, of which waited for: 7 -> 0; matrix products, arithmetic and copies ran while one was open for 10% -> 0% of each run, Pallas kernels for 0% -> 0%
where the time goes in v1:
time: 37.5 us; the launch traced here: 37 us
  Pallas kernels  29.6 us (79%)
  local copies, waits for them, and re-layouts  7.4 us (20%)
    pallas_call x1, Pallas kernels, body(): pl.pallas_call(functools.partial(kernel, (n_sec, n_row, n_rad, nv, nx, nr...  29.6 us
    unnamed x26, local copies, waits for them, and re-layouts  7.4 us

profile of v1, /device:TPU:0, one launch (start us, length us, event | category | flops | bytes accessed | tf_op | source)
XLA Modules:
  0.0 37.0 jit_solution(14582967258610373955)
XLA Ops:
  0.0 0.0 copy-start.6
  0.0 0.0 copy-start.8
  0.0 0.0 copy-start.9
  0.0 0.0 copy-start.10
  0.0 0.0 copy-start.11
  0.0 0.8 %copy.14.matrix = f32[1,3,5,5]{3,2,1,0:T(8,128)S(1)} copy(f32[1,3,5,5]{3,0,2,1:T(1,128)} %param.19) | data formatting | bytes 600 | tf_op args[6]
  0.8 0.0 copy-done.6
  0.8 0.0 copy-done.8
  0.8 0.0 copy-done.9
  0.8 0.0 copy-done.10
  0.8 0.0 copy-done.11
  0.8 0.0 copy-start
  0.8 1.0 %copy-done = f32[5,1,16,8,128]{4,3,2,1,0:T(8,128)S(1)} copy-done((f32[5,1,16,8,128]{4,3,2,1,0:T(8,128)S(1)}, f32[5,1,16,8,128]{4,3,2,1,0:T(8,128)}, u32[]{:S(2)}) %copy-start) | copy-done | bytes 327704
  1.8 0.0 copy-start.1
  1.8 0.8 %copy-done.1 = f32[1,16,8,128]{3,2,1,0:T(8,128)S(1)} copy-done((f32[1,16,8,128]{3,2,1,0:T(8,128)S(1)}, f32[1,16,8,128]{3,2,1,0:T(8,128)}, u32[]{:S(2)}) %copy-start.1) | copy-done | bytes 65560
  2.6 0.0 copy-start.2
  2.6 0.8 %copy-done.2 = f32[1,16,8,128]{3,2,1,0:T(8,128)S(1)} copy-done((f32[1,16,8,128]{3,2,1,0:T(8,128)S(1)}, f32[1,16,8,128]{3,2,1,0:T(8,128)}, u32[]{:S(2)}) %copy-start.2) | copy-done | bytes 65560
  3.5 0.0 copy-start.3
  3.5 0.8 %copy-done.3 = f32[1,16,8,128]{3,2,1,0:T(8,128)S(1)} copy-done((f32[1,16,8,128]{3,2,1,0:T(8,128)S(1)}, f32[1,16,8,128]{3,2,1,0:T(8,128)}, u32[]{:S(2)}) %copy-start.3) | copy-done | bytes 65560
  4.3 0.0 copy-start.4
  4.3 0.8 %copy-done.4 = f32[1,16,8,128]{3,2,1,0:T(8,128)S(1)} copy-done((f32[1,16,8,128]{3,2,1,0:T(8,128)S(1)}, f32[1,16,8,128]{3,2,1,0:T(8,128)}, u32[]{:S(2)}) %copy-start.4) | copy-done | bytes 65560
  5.1 0.0 copy-start.5
  5.1 0.8 %copy-done.5 = f32[1,16,8,128]{3,2,1,0:T(8,128)S(1)} copy-done((f32[1,16,8,128]{3,2,1,0:T(8,128)S(1)}, f32[1,16,8,128]{3,2,1,0:T(8,128)}, u32[]{:S(2)}) %copy-start.5) | copy-done | bytes 65560
  6.0 0.0 copy-start.7
  6.0 0.7 %copy-done.7 = f32[5,8,128]{2,1,0:T(8,128)S(1)} copy-done((f32[5,8,128]{2,1,0:T(8,128)S(1)}, f32[5,8,128]{2,1,0:T(8,128)}, u32[]{:S(2)}) %copy-start.7) | copy-done | bytes 20504
  6.7 29.6 %coupled_steps.1 = f32[640,128]{1,0:T(8,128)S(1)} custom-call(f32[640,128]{1,0:T(8,128)S(1)} %bitcast.12, f32[128,128]{1,0:T(8,128)S(1)} %bitcast.13, f32[128,128]{1,0:T(8,128)S(1)} %bitcast.14, f32[128,128]{1,0:T(8,128)S(1)} %bitcast.15, f32[128,128]{1,0:T(8,128)S(1)} %bitcast.16, f32[128,128]{1,0:T(8,128)S(1)} %bitcast.17, ...), custom_call_target="tpu_custom_call" | custom-call | tf_op jit(solution)/shard_map/coupled_steps/pallas_call | solution.py:554
  36.3 0.7 %copy.17 = f32[5,1,16,8,128]{4,3,2,1,0:T(8,128)} copy(f32[5,1,16,8,128]{4,3,2,1,0:T(8,128)S(1)} %bitcast.11) | data formatting | bytes 655360
Async XLA Ops:
  0.0 0.8 %copy-start.6 = (f32[5,8,128]{2,1,0:T(8,128)S(1)}, f32[5,8,128]{2,1,0:T(8,128)}, u32[]{:S(2)}) copy-start(f32[5,8,128]{2,1,0:T(8,128)} %param.20) | copy-start | bytes 61444
  0.0 0.8 %copy-start.8 = (s32[1,8]{1,0:T(1,128)S(1)}, s32[1,8]{1,0:T(1,128)}, u32[]{:S(2)}) copy-start(s32[1,8]{1,0:T(1,128)} %down.1) | copy-start | bytes 100
  0.0 0.8 %copy-start.9 = (s32[1,8]{1,0:T(1,128)S(1)}, s32[1,8]{1,0:T(1,128)}, u32[]{:S(2)}) copy-start(s32[1,8]{1,0:T(1,128)} %up.1) | copy-start | bytes 100
  0.0 0.8 %copy-start.10 = (f32[5]{0:T(128)S(1)}, f32[5]{0:T(128)}, u32[]{:S(2)}) copy-start(f32[5]{0:T(128)} %weight.1) | copy-start | bytes 64
  0.0 0.8 %copy-start.11 = (f32[5]{0:T(128)S(1)}, f32[5]{0:T(128)}, u32[]{:S(2)}) copy-start(f32[5]{0:T(128)} %coupling.1) | copy-start | bytes 64
  0.8 1.0 %copy-start = (f32[5,1,16,8,128]{4,3,2,1,0:T(8,128)S(1)}, f32[5,1,16,8,128]{4,3,2,1,0:T(8,128)}, u32[]{:S(2)}) copy-start(f32[5,1,16,8,128]{4,3,2,1,0:T(8,128)} %param.13) | copy-start | bytes 983044
  1.8 0.8 %copy-start.1 = (f32[1,16,8,128]{3,2,1,0:T(8,128)S(1)}, f32[1,16,8,128]{3,2,1,0:T(8,128)}, u32[]{:S(2)}) copy-start(f32[1,16,8,128]{3,2,1,0:T(8,128)} %param.14) | copy-start | bytes 196612
  2.6 0.8 %copy-start.2 = (f32[1,16,8,128]{3,2,1,0:T(8,128)S(1)}, f32[1,16,8,128]{3,2,1,0:T(8,128)}, u32[]{:S(2)}) copy-start(f32[1,16,8,128]{3,2,1,0:T(8,128)} %param.15) | copy-start | bytes 196612
  3.5 0.8 %copy-start.3 = (f32[1,16,8,128]{3,2,1,0:T(8,128)S(1)}, f32[1,16,8,128]{3,2,1,0:T(8,128)}, u32[]{:S(2)}) copy-start(f32[1,16,8,128]{3,2,1,0:T(8,128)} %param.16) | copy-start | bytes 196612
  4.3 0.8 %copy-start.4 = (f32[1,16,8,128]{3,2,1,0:T(8,128)S(1)}, f32[1,16,8,128]{3,2,1,0:T(8,128)}, u32[]{:S(2)}) copy-start(f32[1,16,8,128]{3,2,1,0:T(8,128)} %param.17) | copy-start | bytes 196612
  5.1 0.8 %copy-start.5 = (f32[1,16,8,128]{3,2,1,0:T(8,128)S(1)}, f32[1,16,8,128]{3,2,1,0:T(8,128)}, u32[]{:S(2)}) copy-start(f32[1,16,8,128]{3,2,1,0:T(8,128)} %param.18) | copy-start | bytes 196612
  6.0 0.7 %copy-start.7 = (f32[5,8,128]{2,1,0:T(8,128)S(1)}, f32[5,8,128]{2,1,0:T(8,128)}, u32[]{:S(2)}) copy-start(f32[5,8,128]{2,1,0:T(8,128)} %param.21) | copy-start | bytes 61444

commit v2 on v1

--- a/solution.py
+++ b/solution.py
@@ -18,6 +18,20 @@
 
 def kernel(
     sizes,
+    state_hbm,
+    volume_hbm,
+    face_axial_hbm,
+    face_radial_hbm,
+    face_circum_hbm,
+    viscosity_hbm,
+    matrix_hbm,
+    inflow,
+    outflow_hbm,
+    down_hbm,
+    up_hbm,
+    weight_hbm,
+    coupling_hbm,
+    out,
     state,
     volume,
     face_axial,
@@ -25,13 +39,12 @@
     face_circum,
     viscosity,
     matrix,
-    inflow,
     outflow,
     down,
     up,
     weight,
     coupling,
-    out,
+    loaded,
     field,
     coef,
     flow,
@@ -101,6 +114,28 @@
             return pl.ds(index * nr, nr)
         return pl.ds(pl.multiple_of(index * nr, nr), nr)
 
+    loads = [
+        pltpu.make_async_copy(src, dst, loaded.at[i])
+        for i, (src, dst) in enumerate(
+            (
+                (state_hbm, state),
+                (viscosity_hbm, viscosity),
+                (face_circum_hbm, face_circum),
+                (face_radial_hbm, face_radial),
+                (weight_hbm, weight),
+                (outflow_hbm, outflow),
+                (volume_hbm, volume),
+                (face_axial_hbm, face_axial),
+                (up_hbm, up),
+                (coupling_hbm, coupling),
+                (matrix_hbm, matrix),
+                (down_hbm, down),
+            )
+        )
+    ]
+    for load in loads:
+        load.start()
+
     barrier = pltpu.get_barrier_semaphore()
 
     def greet(to):
@@ -133,38 +168,7 @@
     def _():
         each(lambda index: greet(device(sec, index)), True)
 
-    def pressure_of(values):
-        total = weight[0] * values[0]
-        for v in range(1, nv):
-            total = total + weight[v] * values[v]
-        return total
-
-    press_send[0] = pressure_of([state[rows(v * nx)] for v in range(nv)])
-    press_send[STEPS] = pressure_of([outflow[rows(v)] for v in range(nv)])
-    for v in range(nv):
-        flow_send[0, rows(v)] = state[rows(v * nx + nx - 1)]
-
-    def pack_one(packs, value, index):
-        to_left, to_right = packs
-        to_left = jnp.where(lane == index, pltpu.roll(value, index, 1), to_left)
-        to_right = jnp.where(lane == index, pltpu.roll(value, index + 1, 1), to_right)
-        return to_left, to_right
-
     blank = jnp.zeros((nr, lanes), jnp.float32)
-
-    def pack_start(x, packs):
-        for v in range(nv):
-            packs = pack_one(packs, state[rows(v * nx + x)], v * nx + x)
-        packs = pack_one(packs, viscosity[rows(x)], planes + x)
-        return pack_one(packs, face_circum[rows(x)], planes + nx + x)
-
-    packs = lax.fori_loop(0, nx, pack_start, (blank, blank))
-    row_out[0, 0, 0] = packs[0]
-    row_out[0, 0, 1] = packs[1]
-    for side, edge in ((0, 0), (1, nr - 1)):
-        rad_out[0, side, pl.ds(0, planes)] = state[pl.ds(edge, planes, stride=nr)]
-        rad_out[0, side, pl.ds(planes, nx)] = viscosity[pl.ds(edge, nx, stride=nr)]
-        rad_out[0, side, pl.ds(planes + nx, nx)] = face_radial[pl.ds(edge, nx, stride=nr)]
     for v in range(nv):
         for slot in range(2):
             field[slot, rows(v * nx)] = blank
@@ -183,6 +187,38 @@
         for step in range(STEPS):
             rad_in[step, 1] = jnp.zeros(rad_in.shape[2:], jnp.float32)
             rad_in0[step, 1] = blank
+
+    def pressure_of(values):
+        total = weight[0] * values[0]
+        for v in range(1, nv):
+            total = total + weight[v] * values[v]
+        return total
+
+    def pack_one(packs, value, index):
+        to_left, to_right = packs
+        to_left = jnp.where(lane == index, pltpu.roll(value, index, 1), to_left)
+        to_right = jnp.where(lane == index, pltpu.roll(value, index + 1, 1), to_right)
+        return to_left, to_right
+
+    def pack_start(x, packs):
+        for v in range(nv):
+            packs = pack_one(packs, state[rows(v * nx + x)], v * nx + x)
+        packs = pack_one(packs, viscosity[rows(x)], planes + x)
+        return pack_one(packs, face_circum[rows(x)], planes + nx + x)
+
+    for load in loads[:6]:
+        load.wait()
+    press_send[0] = pressure_of([state[rows(v * nx)] for v in range(nv)])
+    press_send[STEPS] = pressure_of([outflow[rows(v)] for v in range(nv)])
+    for v in range(nv):
+        flow_send[0, rows(v)] = state[rows(v * nx + nx - 1)]
+    for side, edge in ((0, 0), (1, nr - 1)):
+        rad_out[0, side, pl.ds(0, planes)] = state[pl.ds(edge, planes, stride=nr)]
+        rad_out[0, side, pl.ds(planes, nx)] = viscosity[pl.ds(edge, nx, stride=nr)]
+        rad_out[0, side, pl.ds(planes + nx, nx)] = face_radial[pl.ds(edge, nx, stride=nr)]
+    packs = lax.fori_loop(0, nx, pack_start, (blank, blank), unroll=True)
+    row_out[0, 0, 0] = packs[0]
+    row_out[0, 0, 1] = packs[1]
 
     one = jnp.int32(1)
     zero = jnp.int32(0)
@@ -288,8 +324,6 @@
 
     send_flow(0)
 
-    wait_beside(0, 0)
-
     def lower_lane(value, packed, index):
         return jnp.where(
             lane == 0, pltpu.roll(packed, lax.rem(lanes - index, lanes), 1), pltpu.roll(value, 1, 1)
@@ -310,47 +344,54 @@
 
     wall = jnp.logical_and(casing, sub == nr - 1)
 
-    def prepare(x, carry):
+    def put_direction(x, d, half, mu, lower, upper):
+        area_l, mu_l = lower
+        area_u, mu_u = upper
+        mix_l, mix_u = half * area_l, half * area_u
+        spread_l, spread_u = mix_l * (mu_l + mu), mix_u * (mu_u + mu)
+        coef[5 * d, rows(x)] = mix_u
+        coef[5 * d + 1, rows(x)] = mix_u - mix_l
+        coef[5 * d + 2, rows(x)] = mix_l
+        coef[5 * d + 3, rows(x)] = spread_u
+        coef[5 * d + 4, rows(x)] = spread_l
+        return spread_l + spread_u
+
+    def prepare_axial(x, carry):
         below, above = jnp.maximum(x - 1, 0), jnp.minimum(x + 1, nx - 1)
-        scale = time_step / volume[rows(x)]
-        half = 0.5 * scale
+        half = (0.5 * time_step) / volume[rows(x)]
+        lower = face_axial[rows(below)], viscosity[rows(below)]
+        upper = face_axial[rows(x)], viscosity[rows(above)]
+        leaves = put_direction(x, 0, half, viscosity[rows(x)], lower, upper)
+        coef[N_COEF - 1, rows(x)] = 1.0 - leaves
+        coef[N_COEF, rows(x)] = half
+        return carry
+
+    def prepare_beside(x, carry):
+        half = coef[N_COEF, rows(x)]
         mu = viscosity[rows(x)]
-        area = face_radial[rows(x)]
-        area = jnp.where(wall, 0.0, area)
+        area = jnp.where(wall, 0.0, face_radial[rows(x)])
         around = face_circum[rows(x)]
         from_left, from_right = row_in[0, 0, 0], row_in[0, 0, 1]
         lower = (
-            (face_axial[rows(below)], viscosity[rows(below)]),
-            (
-                lower_sub(area, rad_in[0, 0, pl.ds(planes + nx + x, 1)]),
-                lower_sub(mu, rad_in[0, 0, pl.ds(planes + x, 1)]),
-            ),
-            (
-                lower_lane(around, from_left, planes + nx + x),
-                lower_lane(mu, from_left, planes + x),
-            ),
-        )
-        upper = (
-            (face_axial[rows(x)], viscosity[rows(above)]),
-            (area, upper_sub(mu, rad_in[0, 1, pl.ds(planes + x, 1)])),
-            (around, upper_lane(mu, from_right, planes + x)),
-        )
-        keep = jnp.ones_like(mu)
-        for d in range(3):
-            area_l, mu_l = lower[d]
-            area_u, mu_u = upper[d]
-            mix_l, mix_u = half * area_l, half * area_u
-            spread_l, spread_u = mix_l * (mu_l + mu), mix_u * (mu_u + mu)
-            keep = keep - (spread_l + spread_u)
-            coef[5 * d, rows(x)] = mix_u
-            coef[5 * d + 1, rows(x)] = mix_u - mix_l
-            coef[5 * d + 2, rows(x)] = mix_l
-            coef[5 * d + 3, rows(x)] = spread_u
-            coef[5 * d + 4, rows(x)] = spread_l
-        coef[N_COEF - 1, rows(x)] = keep
+            lower_sub(area, rad_in[0, 0, pl.ds(planes + nx + x, 1)]),
+            lower_sub(mu, rad_in[0, 0, pl.ds(planes + x, 1)]),
+        )
+        upper = area, upper_sub(mu, rad_in[0, 1, pl.ds(planes + x, 1)])
+        leaves = put_direction(x, 1, half, mu, lower, upper)
+        lower = (
+            lower_lane(around, from_left, planes + nx + x),
+            lower_lane(mu, from_left, planes + x),
+        )
+        upper = around, upper_lane(mu, from_right, planes + x)
+        leaves = leaves + put_direction(x, 2, half, mu, lower, upper)
+        coef[N_COEF - 1, rows(x)] = coef[N_COEF - 1, rows(x)] - leaves
         return carry
 
-    lax.fori_loop(0, nx, prepare, 0)
+    for load in loads[6:]:
+        load.wait()
+    lax.fori_loop(0, nx, prepare_axial, 0, unroll=True)
+    wait_beside(0, 0)
+    prepare_beside(nx - 1, 0)
 
     def advance(x, centre, before, after, packed, edge_rows):
         from_left, from_right = packed
@@ -375,7 +416,7 @@
             total = None
             for d in range(3):
                 for v in range(nv):
-                    term = matrix[0, d, u, v] * mixed[3 * v + d]
+                    term = matrix[d * nv + u, 0, v] * mixed[3 * v + d]
                     total = term if total is None else total + term
             result.append(fresh[u] - total)
         return result
@@ -416,14 +457,12 @@
             keep_plane(x, values)
             return pack_plane(x, values, packs)
 
-        def inside_two(i, packs):
-            x = 1 + 2 * i
-            return inside(x + 1, inside(x, packs))
-
-        pairs = (nx - 2) // 2
-        packs = lax.fori_loop(0, pairs, inside_two, (blank, blank))
-        for x in range(1 + 2 * pairs, nx - 1):
-            packs = inside(x, packs)
+        def all_inside(packs):
+            return lax.fori_loop(1, nx - 1, inside, packs, unroll=True)
+
+        packs = blank, blank
+        if step:
+            packs = all_inside(packs)
 
         def take_press(step=step):
             wait(press[step], press_rs.at[step])
@@ -448,6 +487,10 @@
             for v in range(nv):
                 flow_send[step + 1, rows(v)] = values[v]
             send_flow(step + 1)
+        if step == 0:
+            lax.fori_loop(0, nx - 1, prepare_beside, 0, unroll=True)
+            packs = all_inside(packs)
+        if not final:
             packs = pack_plane(nx - 1, values, packs)
             row_out[step + 1, 0, 0] = packs[0]
             row_out[step + 1, 0, 1] = packs[1]
@@ -550,15 +593,23 @@
 
     dma = pltpu.SemaphoreType.DMA
     in_vmem = pl.BlockSpec(memory_space=pltpu.VMEM)
-    in_smem = pl.BlockSpec(memory_space=pltpu.SMEM)
     result = pl.pallas_call(
         functools.partial(kernel, (n_sec, n_row, n_rad, nv, nx, nr, lanes)),
-        out_shape=jax.ShapeDtypeStruct((planes * nr, lanes), jnp.float32),
-        in_specs=[in_vmem] * 6 + [in_smem] + [in_vmem] * 2 + [in_smem] * 4,
+        out_shape=pltpu.VMEM((planes * nr, lanes), jnp.float32),
+        in_specs=[pl.BlockSpec(memory_space=pltpu.HBM)] * 13,
         out_specs=in_vmem,
         scratch_shapes=[
+            vmem(planes * nr, lanes),
+            *[vmem(nx * nr, lanes)] * 5,
+            pltpu.SMEM((3 * nv, 1, nv), jnp.float32),
+            vmem(block, lanes),
+            pltpu.SMEM(down_donors.shape, jnp.int32),
+            pltpu.SMEM(up_donors.shape, jnp.int32),
+            pltpu.SMEM(pressure_weight.shape, jnp.float32),
+            pltpu.SMEM(boundary_coupling.shape, jnp.float32),
+            dma((12,)),
             vmem(2, planes * nr, lanes),
-            vmem(N_COEF, nx * nr, lanes),
+            vmem(N_COEF + 1, nx * nr, lanes),
             [vmem(group, block, lanes)] * STEPS,
             vmem(STEPS, block, lanes),
             [vmem(group, nr, lanes)] * STEPS,
@@ -582,7 +633,7 @@
             dma((STEPS, 2, 2)),
         ],
         compiler_params=pltpu.CompilerParams(
-            collective_id=0, has_side_effects=True, vmem_limit_bytes=32 * 1024 * 1024
+            collective_id=0, has_side_effects=True, vmem_limit_bytes=60 * 1024 * 1024
         ),
         name="coupled_steps",
     )(
@@ -592,7 +643,7 @@
         flat(face_radial),
         flat(face_circum),
         flat(viscosity),
-        flux_matrix,
+        flux_matrix.transpose(1, 2, 0, 3).reshape(3 * nv, 1, nv),
         flat(inflow_plane),
         flat(outflow_plane),
         down_donors,

time: 37.5 us -> 28.6 us (0.76)
  local copies, waits for them, and re-layouts: 7.4 us -> 0.73 us
  Pallas kernels: 29.6 us -> 27.7 us
    unnamed x26 -> x1, local copies, waits for them, and re-layouts: 7.4 us -> 0.73 us
    pallas_call x1, Pallas kernels: 29.6 us -> 27.7 us  [body(): pl.pallas_call(functools.partial(kernel, (n_sec, n_row, n_rad, nv, nx, nr...]
where the time goes in v2:
time: 28.6 us; the launch traced here: 28.4 us
  Pallas kernels  27.7 us (97%)
  local copies, waits for them, and re-layouts  0.73 us (3%)
    pallas_call x1, Pallas kernels, body(): pl.pallas_call(functools.partial(kernel, (n_sec, n_row, n_rad, nv, nx, nr...  27.7 us
    unnamed x1, local copies, waits for them, and re-layouts  0.73 us

profile of v2, /device:TPU:0, one launch (start us, length us, event | category | flops | bytes accessed | tf_op | source)
XLA Modules:
  0.0 28.4 jit_solution(10407800173711879682)
XLA Ops:
  0.0 27.7 %coupled_steps.1 = f32[640,128]{1,0:T(8,128)S(1)} custom-call(f32[640,128]{1,0:T(8,128)} %bitcast.13, f32[128,128]{1,0:T(8,128)} %bitcast.14, f32[128,128]{1,0:T(8,128)} %bitcast.15, f32[128,128]{1,0:T(8,128)} %bitcast.16, f32[128,128]{1,0:T(8,128)} %bitcast.17, f32[128,128]{1,0:T(8,128)} %bitcast.18, f32[15,1,5]{2,1,0:T(1,128)} %bitcast.21, ...), custom_call_target="tpu_custom_call" | custom-call | tf_op jit(solution)/shard_map/coupled_steps/pallas_call | solution.py:596
  27.7 0.7 %copy.23 = f32[5,1,16,8,128]{4,3,2,1,0:T(8,128)} copy(f32[5,1,16,8,128]{4,3,2,1,0:T(8,128)S(1)} %bitcast.12) | data formatting | bytes 655360

commit v3 on v2

--- a/solution.py
+++ b/solution.py
@@ -53,6 +53,7 @@
     press_send,
     ghost,
     mapped,
+    base,
     row_in,
     row_out,
     rad_in,
@@ -61,6 +62,8 @@
     rad_out0,
     flow_ss,
     flow_rs,
+    pass_ss,
+    pass_rs,
     press_ss,
     press_rs,
     edge_ss,
@@ -72,7 +75,6 @@
     n_sec, n_row, n_rad, nv, nx, nr, lanes = sizes
     group = n_row * n_rad
     planes = nv * nx
-    block = nv * nr
     sec, row, rad = lax.axis_index("sec"), lax.axis_index("row"), lax.axis_index("rad")
     mine = row * n_rad + rad
     first, last = sec == 0, sec == n_sec - 1
@@ -95,6 +97,32 @@
                 one(i)
         else:
             pl.loop(start, group)(one)
+
+    half_group = group // 2
+    parity = lax.rem(row, 2)
+    pair = row + 1 - 2 * parity
+    spot = lax.div(row, 2) * n_rad + rad
+
+    def alike(index):
+        return {
+            "row": 2 * lax.div(index, n_rad) + parity,
+            "rad": lax.rem(index, n_rad),
+        }
+
+    def each_alike(action, skip_self=False):
+        def one(i):
+            action(alike(lax.rem(spot + i, half_group)))
+
+        start = 1 if skip_self else 0
+        if group <= 16:
+            for i in range(start, half_group):
+                one(i)
+        else:
+            pl.loop(start, half_group)(one)
+
+    def slot_of(owner):
+        across, along = lax.div(owner, n_rad), lax.rem(owner, n_rad)
+        return lax.rem(across, 2) * half_group + lax.div(across, 2) * n_rad + along
 
     def send(src, dst, send_sem, recv_sem, to):
         pltpu.make_async_remote_copy(
@@ -230,15 +258,31 @@
     def send_flow(step):
         @pl.when(jnp.logical_not(last))
         def _():
-            each(
-                lambda index: send(
+            each_alike(
+                lambda to: send(
                     flow_send.at[step],
-                    flow[step].at[mine],
+                    flow[step].at[parity * half_group + spot],
                     flow_ss.at[step],
                     flow_rs.at[step],
-                    device(sec + 1, index),
+                    {"sec": sec + 1, **to},
                 )
             )
+
+    def halves(step):
+        own = flow[step].at[pl.ds(parity * half_group, half_group)]
+        other = flow[step].at[pl.ds((1 - parity) * half_group, half_group)]
+        return own, other
+
+    def pass_flow(step):
+        def go():
+            own, _ = halves(step)
+            wait(own, flow_rs.at[step])
+            send(own, own, pass_ss.at[step], pass_rs.at[step], {"row": pair})
+
+        if step:
+            pl.when(jnp.logical_not(first))(go)
+        else:
+            go()
 
     def send_press(step):
         @pl.when(jnp.logical_not(first))
@@ -314,13 +358,11 @@
 
     @pl.when(first)
     def _():
-        each(
-            lambda index: send(
-                inflow, flow[0].at[mine], edge_ss.at[0], flow_rs.at[0], device(sec, index)
-            ),
-            True,
-        )
-        pltpu.make_async_copy(inflow, flow[0].at[mine], flow_rs.at[0]).start()
+        place = flow[0].at[parity * half_group + spot]
+        each_alike(
+            lambda to: send(inflow, place, edge_ss.at[0], flow_rs.at[0], to), True
+        )
+        pltpu.make_async_copy(inflow, place, flow_rs.at[0]).start()
 
     send_flow(0)
 
@@ -402,14 +444,20 @@
             mid = centre[v]
             below, above = edge_rows(v)
             pairs = (
-                (before[v], after[v]),
+                (before and before[v], after and after[v]),
                 (lower_sub(mid, below), upper_sub(mid, above)),
                 (lower_lane(mid, from_left, index), upper_lane(mid, from_right, index)),
             )
             kept = c[N_COEF - 1] * mid
             for d, (lo, hi) in enumerate(pairs):
-                mixed.append(c[5 * d] * hi + c[5 * d + 1] * mid - c[5 * d + 2] * lo)
-                kept = kept + (c[5 * d + 3] * hi + c[5 * d + 4] * lo)
+                mix = c[5 * d + 1] * mid
+                if hi is not None:
+                    mix = mix + c[5 * d] * hi
+                    kept = kept + c[5 * d + 3] * hi
+                if lo is not None:
+                    mix = mix - c[5 * d + 2] * lo
+                    kept = kept + c[5 * d + 4] * lo
+                mixed.append(mix)
             fresh.append(kept)
         result = []
         for u in range(nv):
@@ -421,6 +469,23 @@
             result.append(fresh[u] - total)
         return result
 
+    def complete(x, ghosts, mix_at, keep_at):
+        mix, spread = coef[mix_at, rows(x)], coef[keep_at, rows(x)]
+        mixed = [mix * ghosts[v] for v in range(nv)]
+        result = []
+        for u in range(nv):
+            total = matrix[u, 0, 0] * mixed[0]
+            for v in range(1, nv):
+                total = total + matrix[u, 0, v] * mixed[v]
+            if mix_at == 0:
+                total = -total
+            result.append((base[rows(u)] + spread * ghosts[u]) + total)
+        return result
+
+    def keep_base(values):
+        for v in range(nv):
+            base[rows(v)] = values[v]
+
     for step in range(STEPS):
         final = step == STEPS - 1
         src = state if step == 0 else field.at[(step - 1) % 2]
@@ -464,12 +529,20 @@
         if step:
             packs = all_inside(packs)
 
+        centre = plane(nx - 1)
+        packed = row_in[step, 0, 0], row_in[step, 0, 1]
+        keep_base(
+            advance(nx - 1, centre, plane(nx - 2), None, packed, edge_rows_at(nx - 1))
+        )
+        if step:
+            pass_flow(step)
+
         def take_press(step=step):
+            donors = [up[0, a] for a in range(nr)]
+            spots = [(lax.div(donor, nr), lax.rem(donor, nr)) for donor in donors]
             wait(press[step], press_rs.at[step])
-            for a in range(nr):
-                donor = up[0, a]
-                at = pl.ds(lax.rem(donor, nr), 1)
-                mapped[pl.ds(a, 1)] = press[step][lax.div(donor, nr), at]
+            for a, (owner, at) in enumerate(spots):
+                mapped[pl.ds(a, 1)] = press[step][owner, pl.ds(at, 1)]
 
         if step:
             pl.when(jnp.logical_not(last))(take_press)
@@ -478,16 +551,14 @@
         centre = plane(nx - 1)
         gap = mapped[...] - pressure_of(centre)
         after = [centre[v] + coupling[v] * gap for v in range(nv)]
-        packed = row_in[step, 0, 0], row_in[step, 0, 1]
-        values = advance(
-            nx - 1, centre, plane(nx - 2), after, packed, edge_rows_at(nx - 1)
-        )
+        values = complete(nx - 1, after, 0, 3)
         keep_plane(nx - 1, values)
         if not final:
             for v in range(nv):
                 flow_send[step + 1, rows(v)] = values[v]
             send_flow(step + 1)
         if step == 0:
+            pass_flow(0)
             lax.fori_loop(0, nx - 1, prepare_beside, 0, unroll=True)
             packs = all_inside(packs)
         if not final:
@@ -500,16 +571,17 @@
             send_rads(step + 1, 0)
 
         def take_flow(step=step):
-            wait(flow[step], flow_rs.at[step])
-            for a in range(nr):
-                donor = down[0, a]
-                owner, base = lax.div(donor, nr), lax.rem(donor, nr)
+            donors = [down[0, a] for a in range(nr)]
+            spots = [
+                (slot_of(lax.div(donor, nr)), lax.rem(donor, nr)) for donor in donors
+            ]
+            wait(halves(step)[1], pass_rs.at[step])
+            for a, (owner, at) in enumerate(spots):
                 for v in range(nv):
-                    ghost[pl.ds(v * nr + a, 1)] = flow[step][owner, pl.ds(v * nr + base, 1)]
+                    ghost[pl.ds(v * nr + a, 1)] = flow[step][owner, pl.ds(v * nr + at, 1)]
 
         if step:
             wait_beside(step, 1)
-            pl.when(jnp.logical_not(first))(take_flow)
 
             def edge_rows(v, step=step):
                 at = pl.ds(v, 1)
@@ -517,10 +589,13 @@
 
             packed = row_in[step, 1, 0], row_in[step, 1, 1]
         else:
+            edge_rows = edge_rows_at(0)
+        keep_base(advance(0, plane(0), None, plane(1), packed, edge_rows))
+        if step:
+            pl.when(jnp.logical_not(first))(take_flow)
+        else:
             take_flow()
-            edge_rows = edge_rows_at(0)
-        before = [ghost[rows(v)] for v in range(nv)]
-        values = advance(0, plane(0), before, plane(1), packed, edge_rows)
+        values = complete(0, [ghost[rows(v)] for v in range(nv)], 2, 4)
         keep_plane(0, values)
         if not final:
             press_send[step + 1] = pressure_of(values)
@@ -534,6 +609,13 @@
                 rad_out0[step + 1, 1, pl.ds(v, 1)] = values[v][nr - 1 :]
             send_rads(step + 1, 1)
 
+    wait(halves(0)[0], pass_ss.at[0])
+
+    @pl.when(jnp.logical_not(first))
+    def _():
+        for step in range(1, STEPS):
+            wait(halves(step)[0], pass_ss.at[step])
+
     for step in range(STEPS):
         for part in range(2 if step else 1):
             for side, edge in ((0, floor), (1, casing)):
@@ -546,7 +628,7 @@
     @pl.when(jnp.logical_not(last))
     def _():
         for step in range(STEPS):
-            wait(flow[step], flow_ss.at[step])
+            wait(flow[step].at[pl.ds(0, half_group)], flow_ss.at[step])
 
     @pl.when(jnp.logical_not(first))
     def _():
@@ -555,7 +637,7 @@
 
     @pl.when(first)
     def _():
-        wait(flow[0].at[pl.ds(0, group - 1)], edge_ss.at[0])
+        wait(flow[0].at[pl.ds(0, half_group - 1)], edge_ss.at[0])
 
     @pl.when(last)
     def _():
@@ -616,12 +698,15 @@
             vmem(STEPS + 1, nr, lanes),
             vmem(block, lanes),
             vmem(nr, lanes),
+            vmem(block, lanes),
             vmem(STEPS, 2, 2, nr, lanes),
             vmem(STEPS, 2, 2, nr, lanes),
             vmem(STEPS, 2, held, lanes),
             vmem(STEPS, 2, held, lanes),
             vmem(STEPS, 2, nr, lanes),
             vmem(STEPS, 2, nr, lanes),
+            dma((STEPS,)),
+            dma((STEPS,)),
             dma((STEPS,)),
             dma((STEPS,)),
             dma((STEPS,)),

time: 28.6 us -> 27.7 us (0.969)
  Pallas kernels: 27.7 us -> 26.9 us
    pallas_call x1, Pallas kernels: 27.7 us -> 26.9 us  [body(): pl.pallas_call(functools.partial(kernel, (n_sec, n_row, n_rad, nv, nx, nr...]
where the time goes in v3:
time: 27.7 us; the launch traced here: 27.6 us
  Pallas kernels  26.9 us (97%)
  local copies, waits for them, and re-layouts  0.73 us (3%)
    pallas_call x1, Pallas kernels, body(): pl.pallas_call(functools.partial(kernel, (n_sec, n_row, n_rad, nv, nx, nr...  26.9 us
    unnamed x1, local copies, waits for them, and re-layouts  0.73 us

profile of v3, /device:TPU:0, one launch (start us, length us, event | category | flops | bytes accessed | tf_op | source)
XLA Modules:
  0.0 27.6 jit_solution(16710652328753430981)
XLA Ops:
  0.0 26.9 %coupled_steps.1 = f32[640,128]{1,0:T(8,128)S(1)} custom-call(f32[640,128]{1,0:T(8,128)} %bitcast.13, f32[128,128]{1,0:T(8,128)} %bitcast.14, f32[128,128]{1,0:T(8,128)} %bitcast.15, f32[128,128]{1,0:T(8,128)} %bitcast.16, f32[128,128]{1,0:T(8,128)} %bitcast.17, f32[128,128]{1,0:T(8,128)} %bitcast.18, f32[15,1,5]{2,1,0:T(1,128)} %bitcast.21, ...), custom_call_target="tpu_custom_call" | custom-call | tf_op jit(solution)/shard_map/coupled_steps/pallas_call | solution.py:678
  26.9 0.7 %copy.23 = f32[5,1,16,8,128]{4,3,2,1,0:T(8,128)} copy(f32[5,1,16,8,128]{4,3,2,1,0:T(8,128)S(1)} %bitcast.12) | data formatting | bytes 655360

commit v4 on v3

--- a/solution.py
+++ b/solution.py
@@ -201,20 +201,23 @@
         for slot in range(2):
             field[slot, rows(v * nx)] = blank
     for step in range(STEPS):
-        for side in range(2):
-            rad_out0[step, side] = blank
+        for part in range(1, 3):
+            for side in range(2):
+                rad_out0[step, part, side] = blank
 
     @pl.when(floor)
     def _():
         for step in range(STEPS):
             rad_in[step, 0] = jnp.zeros(rad_in.shape[2:], jnp.float32)
-            rad_in0[step, 0] = blank
+            for part in range(1, 3):
+                rad_in0[step, part, 0] = blank
 
     @pl.when(casing)
     def _():
         for step in range(STEPS):
             rad_in[step, 1] = jnp.zeros(rad_in.shape[2:], jnp.float32)
-            rad_in0[step, 1] = blank
+            for part in range(1, 3):
+                rad_in0[step, part, 1] = blank
 
     def pressure_of(values):
         total = weight[0] * values[0]
@@ -309,7 +312,7 @@
 
     def rad_refs(step, part, side):
         if part:
-            return rad_out0.at[step, side], rad_in0.at[step, 1 - side]
+            return rad_out0.at[step, part, side], rad_in0.at[step, part, 1 - side]
         count = planes if step else planes + 2 * nx
         return (
             rad_out.at[step, side, pl.ds(0, count)],
@@ -514,6 +517,31 @@
 
             return edge_rows
 
+        def edge_rows_of(part, step=step):
+            def edge_rows(v):
+                at = pl.ds(v, 1)
+                return rad_in0[step, part, 0, at], rad_in0[step, part, 1, at]
+
+            return edge_rows
+
+        def send_plane(part, x, values, step=step):
+            packs = pack_plane(x, values, (blank, blank))
+            row_out[step + 1, part, 0] = packs[0]
+            row_out[step + 1, part, 1] = packs[1]
+            send_rows(step + 1, part)
+            for v in range(nv):
+                rad_out0[step + 1, part, 0, pl.ds(v, 1)] = values[v][:1]
+                rad_out0[step + 1, part, 1, pl.ds(v, 1)] = values[v][nr - 1 :]
+            send_rads(step + 1, part)
+
+        def send_inside(packs, step=step, dst=dst):
+            row_out[step + 1, 0, 0] = packs[0]
+            row_out[step + 1, 0, 1] = packs[1]
+            send_rows(step + 1, 0)
+            for side, edge in ((0, 0), (1, nr - 1)):
+                rad_out[step + 1, side, pl.ds(0, planes)] = dst[pl.ds(edge, planes, stride=nr)]
+            send_rads(step + 1, 0)
+
         def inside(x, packs):
             packed = row_in[step, 0, 0], row_in[step, 0, 1]
             values = advance(
@@ -528,12 +556,18 @@
         packs = blank, blank
         if step:
             packs = all_inside(packs)
+            if not final:
+                send_inside(packs)
 
         centre = plane(nx - 1)
-        packed = row_in[step, 0, 0], row_in[step, 0, 1]
-        keep_base(
-            advance(nx - 1, centre, plane(nx - 2), None, packed, edge_rows_at(nx - 1))
-        )
+        if step:
+            wait_beside(step, 2)
+            edge_rows = edge_rows_of(2)
+            packed = row_in[step, 2, 0], row_in[step, 2, 1]
+        else:
+            edge_rows = edge_rows_at(nx - 1)
+            packed = row_in[0, 0, 0], row_in[0, 0, 1]
+        keep_base(advance(nx - 1, centre, plane(nx - 2), None, packed, edge_rows))
         if step:
             pass_flow(step)
 
@@ -560,15 +594,9 @@
         if step == 0:
             pass_flow(0)
             lax.fori_loop(0, nx - 1, prepare_beside, 0, unroll=True)
-            packs = all_inside(packs)
+            send_inside(all_inside(packs))
         if not final:
-            packs = pack_plane(nx - 1, values, packs)
-            row_out[step + 1, 0, 0] = packs[0]
-            row_out[step + 1, 0, 1] = packs[1]
-            send_rows(step + 1, 0)
-            for side, edge in ((0, 0), (1, nr - 1)):
-                rad_out[step + 1, side, pl.ds(0, planes)] = dst[pl.ds(edge, planes, stride=nr)]
-            send_rads(step + 1, 0)
+            send_plane(2, nx - 1, values)
 
         def take_flow(step=step):
             donors = [down[0, a] for a in range(nr)]
@@ -583,10 +611,7 @@
         if step:
             wait_beside(step, 1)
 
-            def edge_rows(v, step=step):
-                at = pl.ds(v, 1)
-                return rad_in0[step, 0, at], rad_in0[step, 1, at]
-
+            edge_rows = edge_rows_of(1)
             packed = row_in[step, 1, 0], row_in[step, 1, 1]
         else:
             edge_rows = edge_rows_at(0)
@@ -600,14 +625,7 @@
         if not final:
             press_send[step + 1] = pressure_of(values)
             send_press(step + 1)
-            packs = pack_plane(0, values, (blank, blank))
-            row_out[step + 1, 1, 0] = packs[0]
-            row_out[step + 1, 1, 1] = packs[1]
-            send_rows(step + 1, 1)
-            for v in range(nv):
-                rad_out0[step + 1, 0, pl.ds(v, 1)] = values[v][:1]
-                rad_out0[step + 1, 1, pl.ds(v, 1)] = values[v][nr - 1 :]
-            send_rads(step + 1, 1)
+            send_plane(1, 0, values)
 
     wait(halves(0)[0], pass_ss.at[0])
 
@@ -617,7 +635,7 @@
             wait(halves(step)[0], pass_ss.at[step])
 
     for step in range(STEPS):
-        for part in range(2 if step else 1):
+        for part in range(3 if step else 1):
             for side, edge in ((0, floor), (1, casing)):
                 wait(row_out.at[step, part, side], row_ss.at[step, part, side])
 
@@ -699,12 +717,12 @@
             vmem(block, lanes),
             vmem(nr, lanes),
             vmem(block, lanes),
-            vmem(STEPS, 2, 2, nr, lanes),
-            vmem(STEPS, 2, 2, nr, lanes),
+            vmem(STEPS, 3, 2, nr, lanes),
+            vmem(STEPS, 3, 2, nr, lanes),
             vmem(STEPS, 2, held, lanes),
             vmem(STEPS, 2, held, lanes),
-            vmem(STEPS, 2, nr, lanes),
-            vmem(STEPS, 2, nr, lanes),
+            vmem(STEPS, 3, 2, nr, lanes),
+            vmem(STEPS, 3, 2, nr, lanes),
             dma((STEPS,)),
             dma((STEPS,)),
             dma((STEPS,)),
@@ -712,10 +730,10 @@
             dma((STEPS,)),
             dma((STEPS,)),
             dma((2,)),
-            dma((STEPS, 2, 2)),
-            dma((STEPS, 2, 2)),
-            dma((STEPS, 2, 2)),
-            dma((STEPS, 2, 2)),
+            dma((STEPS, 3, 2)),
+            dma((STEPS, 3, 2)),
+            dma((STEPS, 3, 2)),
+            dma((STEPS, 3, 2)),
         ],
         compiler_params=pltpu.CompilerParams(
             collective_id=0, has_side_effects=True, vmem_limit_bytes=60 * 1024 * 1024

time: 27.7 us -> 27.3 us (0.986)
  Pallas kernels: 26.9 us -> 26.4 us
    pallas_call x1, Pallas kernels: 26.9 us -> 26.4 us  [body(): pl.pallas_call(functools.partial(kernel, (n_sec, n_row, n_rad, nv, nx, nr...]
where the time goes in v4:
time: 27.3 us; the launch traced here: 27.2 us
  Pallas kernels  26.4 us (97%)
  local copies, waits for them, and re-layouts  0.73 us (3%)
    pallas_call x1, Pallas kernels, body(): pl.pallas_call(functools.partial(kernel, (n_sec, n_row, n_rad, nv, nx, nr...  26.4 us
    unnamed x1, local copies, waits for them, and re-layouts  0.73 us

profile of v4, /device:TPU:0, one launch (start us, length us, event | category | flops | bytes accessed | tf_op | source)
XLA Modules:
  0.0 27.2 jit_solution(10396894110515070240)
XLA Ops:
  0.0 26.4 %coupled_steps.1 = f32[640,128]{1,0:T(8,128)S(1)} custom-call(f32[640,128]{1,0:T(8,128)} %bitcast.13, f32[128,128]{1,0:T(8,128)} %bitcast.14, f32[128,128]{1,0:T(8,128)} %bitcast.15, f32[128,128]{1,0:T(8,128)} %bitcast.16, f32[128,128]{1,0:T(8,128)} %bitcast.17, f32[128,128]{1,0:T(8,128)} %bitcast.18, f32[15,1,5]{2,1,0:T(1,128)} %bitcast.21, ...), custom_call_target="tpu_custom_call" | custom-call | tf_op jit(solution)/shard_map/coupled_steps/pallas_call | solution.py:696
  26.4 0.7 %copy.23 = f32[5,1,16,8,128]{4,3,2,1,0:T(8,128)} copy(f32[5,1,16,8,128]{4,3,2,1,0:T(8,128)S(1)} %bitcast.12) | data formatting | bytes 655360

commit v5 on v4

--- a/solution.py
+++ b/solution.py
@@ -247,7 +247,7 @@
         rad_out[0, side, pl.ds(0, planes)] = state[pl.ds(edge, planes, stride=nr)]
         rad_out[0, side, pl.ds(planes, nx)] = viscosity[pl.ds(edge, nx, stride=nr)]
         rad_out[0, side, pl.ds(planes + nx, nx)] = face_radial[pl.ds(edge, nx, stride=nr)]
-    packs = lax.fori_loop(0, nx, pack_start, (blank, blank), unroll=True)
+    packs = lax.fori_loop(0, nx, pack_start, (blank, blank), unroll=4)
     row_out[0, 0, 0] = packs[0]
     row_out[0, 0, 1] = packs[1]
 
@@ -434,7 +434,7 @@
 
     for load in loads[6:]:
         load.wait()
-    lax.fori_loop(0, nx, prepare_axial, 0, unroll=True)
+    lax.fori_loop(0, nx, prepare_axial, 0, unroll=4)
     wait_beside(0, 0)
     prepare_beside(nx - 1, 0)
 
@@ -551,7 +551,7 @@
             return pack_plane(x, values, packs)
 
         def all_inside(packs):
-            return lax.fori_loop(1, nx - 1, inside, packs, unroll=True)
+            return lax.fori_loop(1, nx - 1, inside, packs, unroll=max(1, (nx - 2) // 2))
 
         packs = blank, blank
         if step:
@@ -593,7 +593,7 @@
             send_flow(step + 1)
         if step == 0:
             pass_flow(0)
-            lax.fori_loop(0, nx - 1, prepare_beside, 0, unroll=True)
+            lax.fori_loop(0, nx - 1, prepare_beside, 0, unroll=5)
             send_inside(all_inside(packs))
         if not final:
             send_plane(2, nx - 1, values)

time: 27.3 us -> 27.4 us (level)
  no operation moved by 1% of the time
where the time goes in v5:
time: 27.4 us; the launch traced here: 27.2 us
  Pallas kernels  26.5 us (97%)
  local copies, waits for them, and re-layouts  0.73 us (3%)
    pallas_call x1, Pallas kernels, body(): pl.pallas_call(functools.partial(kernel, (n_sec, n_row, n_rad, nv, nx, nr...  26.5 us
    unnamed x1, local copies, waits for them, and re-layouts  0.73 us

profile of v5, /device:TPU:0, one launch (start us, length us, event | category | flops | bytes accessed | tf_op | source)
XLA Modules:
  0.0 27.2 jit_solution(15649138797185755591)
XLA Ops:
  0.0 26.5 %coupled_steps.1 = f32[640,128]{1,0:T(8,128)S(1)} custom-call(f32[640,128]{1,0:T(8,128)} %bitcast.13, f32[128,128]{1,0:T(8,128)} %bitcast.14, f32[128,128]{1,0:T(8,128)} %bitcast.15, f32[128,128]{1,0:T(8,128)} %bitcast.16, f32[128,128]{1,0:T(8,128)} %bitcast.17, f32[128,128]{1,0:T(8,128)} %bitcast.18, f32[15,1,5]{2,1,0:T(1,128)} %bitcast.21, ...), custom_call_target="tpu_custom_call" | custom-call | tf_op jit(solution)/shard_map/coupled_steps/pallas_call | solution.py:696
  26.5 0.7 %copy.23 = f32[5,1,16,8,128]{4,3,2,1,0:T(8,128)} copy(f32[5,1,16,8,128]{4,3,2,1,0:T(8,128)S(1)} %bitcast.12) | data formatting | bytes 655360
